TPU v7x, 512 devices: a whole 4x8x8 slice. The times are simulated.
512 devices in a mesh: layer: 32 (over x, z), space: 16 (over y, core).
Axes of the slice: x: 4, y: 8, z: 8, core: 2. Of those that a mesh axis runs over, the one named last changes fastest.
Arguments:
- image: bfloat16 [64, 64, 256], P(None, 'space'), may hold values from -6 to 6
- weights: bfloat16 [128, 64, 576], P('layer'), may hold values from -0.25 to 0.25
Outputs:
- states: bfloat16 [32, 64, 64, 256], P('layer', None, 'space')
All inputs are finite; a program needn't handle non-finite values.
Results may differ from a plain program's by a relative error of at most 0.019.
The roundings to bfloat16 on the way count: a program that leaves them out, or rounds other values in their place, can miss the bound.
Values may be sent and summed in bfloat16 or wider, within the bound.
No kernel may reach another device: no remote copies, remote signals or barrier semaphores. Data moves between devices by JAX's collectives and lax.ppermute only.
A program may use at most 64 MiB of HBM per device.

v0:
```python
import jax
import jax.numpy as jnp
from jax import lax
from jax.sharding import PartitionSpec as P

CYCLES = 2


STEP = 0.125


def with_halo(x, sides, width):
    for axis, dim in sides:
        devices, length = (lax.axis_size(axis), x.shape[dim])
        up = [(i, (i + 1) % devices) for i in range(devices - 1)]
        down = [(j, i) for i, j in up]
        last = lax.slice_in_dim(x, length - width, length, axis=dim)
        initial = lax.slice_in_dim(x, 0, width, axis=dim)
        before = lax.ppermute(last, axis, up)
        after = lax.ppermute(initial, axis, down)
        x = jnp.concatenate([before, x, after], axis=dim)
    return x


def from_behind(x, axis, by):
    devices = lax.axis_size(axis)
    pairs = [(i, i + by) for i in range(devices) if 0 <= i + by < devices]
    return lax.ppermute(x, axis, pairs)


def tap_product(padded, kernel):
    height = padded.shape[1] - 2
    width = padded.shape[2]
    wide = jnp.pad(padded, ((0, 0), (0, 0), (1, 1)))
    taps = jnp.concatenate(
        [wide[:, dy : dy + height, dx : dx + width] for dy in range(3) for dx in range(3)], 0
    )
    flat = taps.reshape(taps.shape[0], height * width)
    return jnp.dot(kernel, flat, preferred_element_type=jnp.float32).reshape(
        kernel.shape[0], height, width
    )


def pooled(field):
    chans, height, width = field.shape
    return field.astype(jnp.float32).reshape(chans, height // 2, 2, width // 2, 2).mean(axis=(2, 4))


def widened(field):
    return jnp.repeat(jnp.repeat(field, 2, axis=1), 2, axis=2)


def coarse_step(state, kernel, factor):
    padded = with_halo(state.astype(jnp.bfloat16), (("space", 1),), 1)
    return state + factor * jnp.tanh(tap_product(padded, kernel))


def sweep(start, kernels):

    def single_layer(field, kernel):
        padded = with_halo(field, (("space", 1),), 1)
        return (
            (field.astype(jnp.float32) + STEP * jnp.tanh(tap_product(padded, kernel))).astype(
                jnp.bfloat16
            ),
            None,
        )

    return lax.scan(single_layer, start, kernels)[0]


def per_device(image, weights):
    block_index = lax.axis_index("layer")
    blocks = lax.axis_size("layer")
    factor = weights.shape[0] * STEP
    own_kernel = jnp.mean(weights.astype(jnp.float32), axis=0).astype(jnp.bfloat16)
    start = pooled(image)
    states = image
    for cycle in range(CYCLES):
        ends = sweep(states, weights)
        tau = pooled(ends) - coarse_step(pooled(states), own_kernel, factor)

        def link(step, carry):
            sent = coarse_step(carry, own_kernel, factor) + tau
            received = from_behind(sent, "layer", 1)
            return jnp.where(block_index == 0, start, received)

        level = lax.fori_loop(0, blocks - 1, link, start)
        before = from_behind(ends, "layer", 1)
        fixed = (before.astype(jnp.float32) + widened(level - pooled(before))).astype(jnp.bfloat16)
        states = jnp.where(block_index == 0, image, fixed)
    return states[None]


def solution(mesh):
    in_specs = (P(None, "space", None), P("layer", None, None))
    out_specs = P("layer", None, "space", None)
    return jax.shard_map(
        per_device, mesh=mesh, in_specs=in_specs, out_specs=out_specs, check_vma=False
    )
```

profile of v0, /device:TPU:38, one launch (start us, length us, event | category | flops | bytes accessed | tf_op | source)
XLA Modules:
  0.0 1249.0 jit_solution(893235061764514889)
XLA Ops:
  0.9 41.3 %while.48 = (s32[]{:T(128)}, bf16[64,4,256]{2,0,1:T(8,128)(2,1)S(1)}, bf16[4,64,576]{2,1,0:T(8,128)(2,1)}, s32[]{:T(128)}) while((s32[]{:T(128)}, bf16[64,4,256]{2,0,1:T(8,128)(2,1)S(1)}, bf16[4,64,576]{2,1,0:T(8,128)(2,1)}, s32[]{:T(128)}) %tuple.116), condition=%wide.region_1.0_spmd, body=%wide.region_0.0_spmd.sunk | while | flops 77472768 | bytes 4736657 | solution.py:69
  58.5 568.3 %while.49 = (s32[]{:T(128)}, f32[64,2,128]{2,1,0:T(2,128)S(1)}, pred[]{:T(512)}, bf16[64,576]{1,0:T(8,128)(2,1)S(1)}, f32[64,2,128]{2,1,0:T(2,128)S(1)}, /*index=5*/f32[64,2,128]{2,1,0:T(2,128)S(1)}, s32[]{:T(128)}) while((s32[]{:T(128)}, f32[64,2,128]{2,1,0:T(2,128)S(1)}, pred[]{:T(512)}, bf16[64,576]{1,0:T(8,128)(2,1)S(1)}, ...), condition=%wide.region_6.7_spmd, body=%wide.region_5.6_spmd.sunk | while | flops 19503104 | bytes 2401478 | solution.py:88
  74.1 6.8 collective-permute-done.4
  92.7 6.3 collective-permute-done.4
  110.9 6.3 collective-permute-done.4
  129.1 6.3 collective-permute-done.4
  147.3 6.3 collective-permute-done.4
  165.5 6.3 collective-permute-done.4
  183.7 6.3 collective-permute-done.4
  201.9 6.3 collective-permute-done.4
  220.1 6.3 collective-permute-done.4
  238.3 6.3 collective-permute-done.4
  256.5 6.3 collective-permute-done.4
  274.7 6.3 collective-permute-done.4
  292.9 6.3 collective-permute-done.4
  311.1 6.3 collective-permute-done.4
  329.3 6.3 collective-permute-done.4
  347.5 6.3 collective-permute-done.4
  365.7 6.3 collective-permute-done.4
  383.9 6.3 collective-permute-done.4
  402.1 6.3 collective-permute-done.4
  420.3 6.3 collective-permute-done.4
  438.5 6.3 collective-permute-done.4
  456.7 6.3 collective-permute-done.4
  474.9 6.3 collective-permute-done.4
  493.1 6.3 collective-permute-done.4
  511.3 6.3 collective-permute-done.4
  529.5 6.3 collective-permute-done.4
  547.7 6.3 collective-permute-done.4
  565.9 6.3 collective-permute-done.4
  584.1 6.3 collective-permute-done.4
  602.3 6.3 collective-permute-done.4
  620.5 6.3 collective-permute-done.4
  634.8 37.6 %while.50 = (s32[]{:T(128)}, bf16[64,4,256]{2,0,1:T(8,128)(2,1)S(1)}, bf16[4,64,576]{2,1,0:T(8,128)(2,1)S(1)}, s32[]{:T(128)}) while((s32[]{:T(128)}, bf16[64,4,256]{2,0,1:T(8,128)(2,1)S(1)}, bf16[4,64,576]{2,1,0:T(8,128)(2,1)S(1)}, s32[]{:T(128)}) %tuple.130), condition=%wide.region_9.10_spmd, body=%wide.region_8.9_spmd.sunk | while | flops 77472768 | bytes 4736657 | solution.py:69
  675.9 7.2 collective-permute-done.13
  683.7 564.1 %while.51 = (s32[]{:T(128)}, f32[64,2,128]{2,1,0:T(2,128)S(1)}, pred[]{:T(512)}, bf16[64,576]{1,0:T(8,128)(2,1)S(1)}, f32[64,2,128]{2,1,0:T(2,128)S(1)}, /*index=5*/f32[64,2,128]{2,1,0:T(2,128)S(1)}, s32[]{:T(128)}) while((s32[]{:T(128)}, f32[64,2,128]{2,1,0:T(2,128)S(1)}, pred[]{:T(512)}, bf16[64,576]{1,0:T(8,128)(2,1)S(1)}, ...), condition=%wide.region_13.14_spmd, body=%wide.region_12.13_spmd.sunk | while | flops 19503104 | bytes 2401478 | solution.py:88
  695.5 6.3 collective-permute-done.9
  713.7 6.3 collective-permute-done.9
  731.9 6.3 collective-permute-done.9
  750.1 6.3 collective-permute-done.9
  786.5 6.3 collective-permute-done.9
  859.3 6.3 collective-permute-done.9
  913.9 6.3 collective-permute-done.9
  932.1 6.3 collective-permute-done.9
  986.7 6.3 collective-permute-done.9
  1059.5 6.3 collective-permute-done.9
  1132.3 6.3 collective-permute-done.9
  1205.0 6.3 collective-permute-done.9
  (1528 shorter events, 960.5 us)
Async XLA Ops:
  42.4 15.6 %collective-permute-start.10 = (bf16[64,4,256]{0,2,1:T(8,128)(2,1)S(1)}, bf16[64,4,256]{0,2,1:T(8,128)(2,1)S(1)}, u32[]{:S(2)}, u32[]{:S(2)}) collective-permute-start(bf16[64,4,256]{0,2,1:T(8,128)(2,1)S(1)} %copy.50), channel_id=1, source_target_pairs={{0,16},{16,32},{32,48},{48,64},{64,80},{80,96},{96,112},{112,128},... | collective-permute-start | bytes 393224 | tf_op jit(solution)/shard_map/ppermute | solution.py:28
  69.8 11.1 collective-permute-start.4
  90.8 8.3 collective-permute-start.4
  109.0 8.3 collective-permute-start.4
  127.2 8.3 collective-permute-start.4
  145.4 8.3 collective-permute-start.4
  163.6 8.3 collective-permute-start.4
  181.8 8.3 collective-permute-start.4
  200.0 8.3 collective-permute-start.4
  218.2 8.3 collective-permute-start.4
  236.4 8.3 collective-permute-start.4
  254.6 8.3 collective-permute-start.4
  272.8 8.3 collective-permute-start.4
  291.0 8.3 collective-permute-start.4
  309.2 8.3 collective-permute-start.4
  327.4 8.3 collective-permute-start.4
  345.6 8.3 collective-permute-start.4
  363.8 8.3 collective-permute-start.4
  382.0 8.3 collective-permute-start.4
  400.2 8.3 collective-permute-start.4
  418.4 8.3 collective-permute-start.4
  436.6 8.3 collective-permute-start.4
  454.8 8.3 collective-permute-start.4
  473.0 8.3 collective-permute-start.4
  491.2 8.3 collective-permute-start.4
  509.4 8.3 collective-permute-start.4
  527.6 8.3 collective-permute-start.4
  545.8 8.3 collective-permute-start.4
  564.0 8.3 collective-permute-start.4
  582.2 8.3 collective-permute-start.4
  600.4 8.3 collective-permute-start.4
  618.5 8.3 collective-permute-start.4
  628.0 47.1 %collective-permute-start.14 = (bf16[64,1,128]{2,0,1:T(8,128)(2,1)S(1)}, bf16[64,1,128]{2,0,1:T(8,128)(2,1)S(1)}, u32[]{:S(2)}, u32[]{:S(2)}) collective-permute-start(bf16[64,1,128]{2,0,1:T(8,128)(2,1)S(1)} %get-tuple-element.349), channel_id=1, source_target_pairs={{0,1},{1,2},{2,3},{3,4},{4,5},{5,6},{6,7},{7,8},{8,9},{9,10},{10,1... | collective-permute-start | bytes 49160 | tf_op jit(solution)/shard_map/ppermute | solution.py:19
  629.9 45.2 %collective-permute-start.15 = (bf16[64,1,128]{2,0,1:T(8,128)(2,1)S(1)}, bf16[64,1,128]{2,0,1:T(8,128)(2,1)S(1)}, u32[]{:S(2)}, u32[]{:S(2)}) collective-permute-start(bf16[64,1,128]{2,0,1:T(8,128)(2,1)S(1)} %get-tuple-element.350), channel_id=1, source_target_pairs={{1,0},{2,1},{3,2},{4,3},{5,4},{6,5},{7,6},{8,7},{9,8},{10,9},{11,1... | collective-permute-start | bytes 49160 | tf_op jit(solution)/shard_map/ppermute | solution.py:20
  672.7 10.4 collective-permute-start.13
  693.6 8.3 collective-permute-start.9
  711.8 8.3 collective-permute-start.9
  730.0 8.3 collective-permute-start.9
  784.6 8.3 collective-permute-start.9
  839.2 8.3 collective-permute-start.9
  857.4 8.3 collective-permute-start.9
  911.9 8.3 collective-permute-start.9
  930.1 8.3 collective-permute-start.9
  984.7 8.3 collective-permute-start.9
  1057.5 8.3 collective-permute-start.9
  1130.3 8.3 collective-permute-start.9
  1184.9 8.3 collective-permute-start.9
  1203.1 8.3 collective-permute-start.9
  (162 other events, 977.0 us)
where the time goes:
time: 1250 us
  waiting for transfers between devices  685 us (55%)
  starting transfers between devices  445 us (36%)
  local copies, waits for them, and re-layouts  47.8 us (4%)
  other arithmetic  44.6 us (4%)
  matrix products  18.6 us (1%)
    ppermute x64, waiting for transfers between devices, from_behind(): return lax.ppermute(x, axis, pairs)  402 us
    ppermute x72, waiting for transfers between devices, with_halo(): before = lax.ppermute(last, axis, up)  282 us
    ppermute x72, starting transfers between devices, with_halo(): before = lax.ppermute(last, axis, up)  172 us
    ppermute x72, starting transfers between devices, with_halo(): after = lax.ppermute(initial, axis, down)  146 us
    ppermute x64, starting transfers between devices, from_behind(): return lax.ppermute(x, axis, pairs)  128 us
    while x358, local copies, waits for them, and re-layouts  27.4 us
  transfers between devices with their start and end apart: 208, of which 135 were waited for; matrix products, arithmetic and copies ran while one was open for 1% of the time, Pallas kernels for 0%

commit v1 on v0

v1 whole, which is shorter than its diff:
```python
import functools

import jax
import jax.numpy as jnp
from jax import lax
from jax.experimental import pallas as pl
from jax.experimental.pallas import tpu as pltpu
from jax.sharding import Mesh
from jax.sharding import PartitionSpec as P


STEP = 0.125
C = 64
FU, CU = 22, 11
HEIGHT = 64
FP, CP = 80, 40
FL, CL = 256, 128
OWN = 16
EDGE = 11
WIDTH = 256
BLOCKS = 4
PLANES, ZS, YS = 4, 8, 8
F32, BF16 = jnp.float32, jnp.bfloat16


def unit(u, count=1):
    start = u * C
    if not isinstance(u, int):
        start = pl.multiple_of(start, C)
    return pl.ds(start, count * C)


def lane_of(shape):
    return lax.broadcasted_iota(jnp.int32, shape, 1)


def pool_matrix():
    rows = lax.broadcasted_iota(jnp.int32, (FL, CL), 0)
    return jnp.where((rows >> 1) == lane_of((FL, CL)), 0.25, 0.0).astype(BF16)


def widen_matrix():
    rows = lax.broadcasted_iota(jnp.int32, (CL, FL), 0)
    return jnp.where(rows == (lane_of((CL, FL)) >> 1), 1.0, 0.0).astype(BF16)


def part_of(lane, pitch):
    return (lane >= pitch).astype(jnp.int32) + (lane >= 2 * pitch).astype(jnp.int32)


def within(lane, pitch):
    return lane - pitch * part_of(lane, pitch)


def factors(z, lanes, pitch, edge, own, width, value):
    lane = lane_of((1, lanes))
    column = within(lane, pitch) + (own * z - edge)
    inside = (column >= 0) & (column < width) & (lane < 3 * pitch)
    full = jnp.where(inside, value, 0.0).astype(F32)
    return full, jnp.where(lane < 2 * pitch, full, 0.0)


def fine_factors(z):
    return factors(z, FL, FP, 2 * EDGE, 2 * OWN, WIDTH, STEP)


def coarse_factors(z):
    return factors(z, CL, CP, EDGE, OWN, WIDTH // 2, BLOCKS * STEP)


def dot(a, b):
    return jnp.dot(a, b, preferred_element_type=F32)


def shifted_sum(product):
    lanes = product.shape[1]
    return pltpu.roll(product[:C], 1, 1) + product[C : 2 * C] + pltpu.roll(product[2 * C :], lanes - 1, 1)


def arranged(kernel):
    return jnp.concatenate(
        [
            jnp.concatenate(
                [kernel[:, (3 * dy + dx) * C : (3 * dy + dx + 1) * C] for dy in range(3)], axis=1
            )
            for dx in range(3)
        ],
        axis=0,
    )


def around(first, last, pitch):
    lanes = first.shape[1]
    lane = lane_of(first.shape)
    front = jnp.where((lane >= pitch) & (lane < 3 * pitch), pltpu.roll(last, pitch, 1), 0.0)
    behind = jnp.where(lane < 2 * pitch, pltpu.roll(first, lanes - pitch, 1), 0.0)
    return front.astype(BF16), behind.astype(BF16)


def fine_halo(ref):
    front, behind = around(ref[unit(1), :].astype(F32), ref[unit(FU), :].astype(F32), FP)
    ref[unit(0), :] = front
    ref[unit(FU + 1), :] = behind


def coarse_halo(ref, first, last):
    front, behind = around(first, last, CP)
    ref[unit(0), :] = front
    ref[unit(CU + 1), :] = behind


CHUNK = 4


def pooled_rows(rows, matrix):
    halves = dot(rows, matrix)
    return [
        halves[2 * i * C : (2 * i + 1) * C] + halves[(2 * i + 1) * C : (2 * i + 2) * C]
        for i in range(rows.shape[0] // (2 * C))
    ]


def corrected(first, second, level, pooled, widen):
    change = level - pooled
    high = change.astype(BF16)
    low = (change - high.astype(F32)).astype(BF16)
    wide = dot(high, widen) + dot(low, widen)
    return (first.astype(F32) + wide).astype(BF16), (second.astype(F32) + wide).astype(BF16)


def states_from_rows(xa, rows, level, pool, widen):
    for u in range(0, CU, CHUNK):
        count = min(CHUNK, CU - u)
        block = rows[0, 2 * u : 2 * u + 2 * count].reshape(2 * count * C, FL)
        for i, pooled in enumerate(pooled_rows(block, pool)):
            one, two = corrected(
                rows[0, 2 * (u + i)], rows[0, 2 * (u + i) + 1], level[0, u + i], pooled, widen
            )
            xa[unit(2 * (u + i) + 1), :] = one
            xa[unit(2 * (u + i) + 2), :] = two


def states_from_tile(xa, tile):
    for u in range(FU):
        xa[unit(u + 1), :] = tile[u]


def pool_states(xa, sp, sb, pool):
    for u in range(0, CU, CHUNK):
        count = min(CHUNK, CU - u)
        for i, s in enumerate(pooled_rows(xa[unit(2 * u + 1, 2 * count), :], pool)):
            sp[u + i] = s
            sb[unit(u + i + 1), :] = s.astype(BF16)
    coarse_halo(sb, sp[0], sp[CU - 1])


def run_layers(wk, xa, xb, mf):
    def layer(l, src, dst):
        kernel = wk[0, l]
        for u in range(FU):
            conv = shifted_sum(dot(kernel, src[unit(u, 3), :]))
            x = src[unit(u + 1), :].astype(F32)
            dst[unit(u + 1), :] = (x + mf[u >= FU - 2] * jnp.tanh(conv)).astype(BF16)
        fine_halo(dst)

    @pl.loop(0, 2)
    def _(t):
        layer(2 * t, xa, xb)
        layer(2 * t + 1, xb, xa)


def write_tau(ck, xa, sp, sb, tau_out, pool, mc):
    kernel = ck[0]
    for u in range(0, CU, CHUNK):
        count = min(CHUNK, CU - u)
        for i, ends in enumerate(pooled_rows(xa[unit(2 * u + 1, 2 * count), :], pool)):
            conv = shifted_sum(dot(kernel, sb[unit(u + i, 3), :]))
            tau_out[0, u + i] = (ends - (sp[u + i] + mc[u + i == CU - 1] * jnp.tanh(conv))).astype(BF16)


def first_kernel(sc, w0, w1, w2, w3, source, tau, ends, wk, ck, last, tile, sp, xa, xb, sb, sem):
    step = pl.program_id(0)
    z = sc[1]
    block = (z + step) & (BLOCKS - 1)
    pool = pool_matrix()

    def take(w):
        for l in range(4):
            wk[0, l] = arranged(w[l])
        total = w[0].astype(F32) + w[1].astype(F32) + w[2].astype(F32) + w[3].astype(F32)
        ck[0] = arranged((total * 0.25).astype(BF16))

    for i, w in enumerate((w0, w1, w2, w3)):
        pl.when(step == i)(functools.partial(take, w))

    @pl.when(step == 0)
    def _():
        zero = jnp.zeros((C, FP), BF16)

        def piece(row):
            if row >= HEIGHT:
                return zero
            strip, i = row // 4, row % 4
            return source[strip, :, i * FP : (i + 1) * FP]

        for u in range(FU):
            parts = [piece(u), piece(FU + u), piece(2 * FU + u), zero[:, : FL - 3 * FP]]
            tile[u] = jnp.concatenate(parts, axis=1)

    states_from_tile(xa, tile)
    fine_halo(xa)
    pl.when(step == 0)(lambda: pool_states(xa, sp, sb, pool))
    run_layers(wk, xa, xb, fine_factors(z))

    def to_last():
        return pltpu.make_async_copy(xa.at[pl.ds(C, FU * C), :], last, sem)

    pl.when(block == BLOCKS - 1)(lambda: to_last().start())
    for u in range(FU):
        ends[0, u] = xa[unit(u + 1), :]
    write_tau(ck, xa, sp, sb, tau, pool, coarse_factors(z))
    pl.when(block == BLOCKS - 1)(lambda: to_last().wait())


def later_kernel(sc, wk, ck, before, level, tau, edge, edge_other, xa, xb, sp, sb):
    z, y, c = sc[1], sc[2], sc[3]
    pool = pool_matrix()
    states_from_rows(xa, before, level, pool, widen_matrix())
    fine_halo(xa)
    pool_states(xa, sp, sb, pool)
    run_layers(wk, xa, xb, fine_factors(z))
    for out, k in ((edge, c), (edge_other, 1 - c)):
        for r in range(4):
            row = 8 * y + 4 * k + r
            out[0, r] = xa[unit(row - FU * part_of(row, FU) + 1), :]
    write_tau(ck, xa, sp, sb, tau, pool, coarse_factors(z))


def whole(shape):
    return pl.BlockSpec(shape, lambda i, s: (0,) * len(shape))


def at_step(shape):
    return pl.BlockSpec((1,) + shape, lambda i, s: (i,) + (0,) * len(shape))


def at_slot(shape, by=0):
    return pl.BlockSpec((1,) + shape, lambda i, s: (((s[1] + i) & (BLOCKS - 1)) + by,) + (0,) * len(shape))


ANY = pl.BlockSpec(memory_space=pl.ANY)
ROWS_AT = 16
TAU = (BLOCKS, CU, C, CL)
ENDS = (BLOCKS + 1, FU, C, FL)
EDGES = (BLOCKS, 4, C, FL)
ROWS = (2 * BLOCKS, 2, C, CL)
TILE = (FU, C, FL)
START = (CU, C, CL)
KERS = (BLOCKS, 4, 3 * C, 3 * C)
KER = (BLOCKS, 3 * C, 3 * C)
LAST = (FU * C, FL)
VMEM_LIMIT = 56 * 1024 * 1024
STATES = [
    pltpu.VMEM(((FU + 2) * C, FL), BF16),
    pltpu.VMEM(((FU + 2) * C, FL), BF16),
]
POOLED = [pltpu.VMEM(((CU + 2) * C, CL), BF16)]


def sweep_cost(count):
    return pl.CostEstimate(
        flops=2 * count * 4 * 192 * 192 * FU * FL,
        bytes_accessed=count * (4 << 20),
        transcendentals=count * 4 * C * FU * FL,
    )


def first_sweeps(place, weights, source):
    return pl.pallas_call(
        first_kernel,
        out_shape=[
            jax.ShapeDtypeStruct(TAU, BF16),
            jax.ShapeDtypeStruct(ENDS, BF16),
            jax.ShapeDtypeStruct(KERS, BF16),
            jax.ShapeDtypeStruct(KER, BF16),
            jax.ShapeDtypeStruct(LAST, BF16),
            jax.ShapeDtypeStruct(TILE, BF16),
            jax.ShapeDtypeStruct(START, F32),
        ],
        grid_spec=pltpu.PrefetchScalarGridSpec(
            num_scalar_prefetch=1,
            grid=(BLOCKS,),
            in_specs=[whole((4, C, 9 * C))] * 4 + [whole((ROWS_AT, C, 4 * FP))],
            out_specs=[
                at_slot(TAU[1:]),
                at_slot(ENDS[1:], 1),
                at_slot(KERS[1:]),
                at_slot(KER[1:]),
                ANY,
                whole(TILE),
                whole(START),
            ],
            scratch_shapes=STATES + POOLED + [pltpu.SemaphoreType.DMA],
        ),
        compiler_params=pltpu.CompilerParams(vmem_limit_bytes=VMEM_LIMIT),
        cost_estimate=sweep_cost(BLOCKS),
    )(place, *weights, source)


def later_sweeps(place, wk, ck, before, levels):
    return pl.pallas_call(
        later_kernel,
        out_shape=[
            jax.ShapeDtypeStruct(TAU, BF16),
            jax.ShapeDtypeStruct(EDGES, BF16),
            jax.ShapeDtypeStruct(EDGES, BF16),
        ],
        grid_spec=pltpu.PrefetchScalarGridSpec(
            num_scalar_prefetch=1,
            grid=(BLOCKS,),
            in_specs=[at_step(KERS[1:]), at_step(KER[1:]), at_step(ENDS[1:]), at_step(TAU[1:])],
            out_specs=[at_step(TAU[1:]), at_step(EDGES[1:]), at_step(EDGES[1:])],
            scratch_shapes=STATES + [pltpu.VMEM(START, F32)] + POOLED,
        ),
        compiler_params=pltpu.CompilerParams(vmem_limit_bytes=VMEM_LIMIT),
        cost_estimate=sweep_cost(BLOCKS),
    )(place, wk, ck, before, levels)


def chain_kernel(plane, ending, sc, below, same, above, start, tau_own, tau_other, ck_own, ck_other, *refs):
    opening = plane == 0
    if opening:
        levels, pack, lf, la, lb, ks, ts, lv, lr, pk, sems, out_sems = refs
    else:
        _, levels, pack, lf, la, lb, ks, ts, lv, lr, pk, sems, out_sems = refs
    x, z, y, c = sc[0], sc[1], sc[2], sc[3]

    def half(h):
        return slice(128 * h, 128 * h + 128)

    def fetches(j, tau, kernel):
        at = j & (BLOCKS - 1)
        return (
            pltpu.make_async_copy(kernel.at[at], ks.at[j], sems.at[2 * BLOCKS + j]),
            pltpu.make_async_copy(tau.at[at], ts.at[j], sems.at[j]),
        )

    def begin(j):
        def start(tau, kernel):
            for copy in fetches(j, tau, kernel):
                copy.start()

        pl.when((j >> 2) == c)(lambda: start(tau_own, ck_own))
        pl.when((j >> 2) != c)(lambda: start(tau_other, ck_other))

    def level_copy(slot):
        return pltpu.make_async_copy(lv.at[slot], levels.at[slot], out_sems.at[slot])

    @pl.when(x == plane)
    def _():
        if opening:
            begin_at = [pltpu.make_async_copy(start, lv.at[BLOCKS], sems.at[4 * BLOCKS])]
        else:
            begin_at = [
                pltpu.make_async_copy(ref, pk.at[i], sems.at[4 * BLOCKS + i])
                for i, ref in enumerate((below, same, above))
            ]
        for copy in begin_at:
            copy.start()
        for j in range(AHEAD):
            begin(j)
        mc = coarse_factors(z)
        lane = within(lane_of((C, CL)), CP)
        inside = lane_of((C, CL)) < 3 * CP
        for copy in begin_at:
            copy.wait()

        def halo_of(ref):
            front, behind = around(lf[unit(0), half(0)], lf[unit(4), half(1)], CP)
            ref[unit(0), half(0)] = front
            ref[unit(0), half(1)] = lf[unit(5), half(0)].astype(BF16)
            ref[unit(7), half(0)] = lf[unit(0), half(1)].astype(BF16)
            ref[unit(6), half(1)] = behind

        def put(u, h, value):
            lf[unit(u), half(h)] = value
            la[unit(u + 1), half(h)] = value.astype(BF16)

        if opening:
            lf[unit(HU - 1), half(1)] = jnp.zeros((C, CL), F32)

            @pl.loop(0, HU)
            def _(u):
                put(u, 0, lv[BLOCKS, u])

            @pl.loop(0, CU - HU)
            def _(u):
                put(u, 1, lv[BLOCKS, HU + u])

        else:

            @pl.loop(0, HU // 2)
            def _(a):
                for h in range(2):
                    pieces = [pk[n, a + h * (HU // 2)].astype(F32) for n in range(3)]
                    for i in range(2):

                        def placed(n, by):
                            return pltpu.roll(pieces[n], (by - 16 * i) % 128, 1)

                        value = jnp.where(lane < EDGE, placed(0, EDGE - 16), placed(1, EDGE))
                        value = jnp.where(lane < EDGE + OWN, value, placed(2, EDGE + 16))
                        put(2 * a + i, h, jnp.where((lane >= 2) & (lane < 36) & inside, value, 0.0))

        halo_of(la)

        def step(j, src, dst):
            own = (j >> 2) == c
            slot = jnp.where(own, j & (BLOCKS - 1), BLOCKS)
            pl.when(j + AHEAD < 2 * BLOCKS)(lambda: begin(j + AHEAD))
            for copy in fetches(j, tau_own, ck_own):
                copy.wait()
            kernel = ks[j]
            if ending:
                for r in range(2):
                    row = 4 * y + 2 * c + r
                    u = row - CU * part_of(row, CU)
                    h = (u >= HU).astype(jnp.int32)
                    rows = lf[unit(u - HU * h), :]
                    lr[j, r] = jnp.where(h == 1, rows[:, half(1)], rows[:, half(0)])
            for u in range(HU):
                product = dot(kernel, src[unit(u, 3), :])
                for h in range(2):
                    if u + HU * h >= CU:
                        continue
                    conv = shifted_sum(product[:, half(h)])
                    old = lf[unit(u), half(h)]
                    if not ending:
                        lv[slot, u + HU * h] = old
                    new = old + mc[u + HU * h == CU - 1] * jnp.tanh(conv) + ts[j, u + HU * h].astype(F32)
                    lf[unit(u), half(h)] = new
                    dst[unit(u + 1), half(h)] = new.astype(BF16)
            halo_of(dst)
            if not ending:
                pl.when(own)(lambda: level_copy(j & (BLOCKS - 1)).start())

        @pl.loop(0, BLOCKS)
        def _(t):
            step(2 * t, la, lb)
            step(2 * t + 1, lb, la)

        @pl.loop(0, HU // 2)
        def _(a):
            for h in range(2):
                total = jnp.zeros((C, CL), F32)
                for i in range(2):
                    moved = pltpu.roll(lf[unit(2 * a + i), half(h)], (16 * i - EDGE) % 128, 1)
                    total = jnp.where((lane >= 16 * i) & (lane < 16 * i + 16), moved, total)
                pk[0, a + h * (HU // 2)] = total.astype(BF16)

        out = pltpu.make_async_copy(pk.at[0], pack, sems.at[4 * BLOCKS])
        out.start()
        if ending:
            rows_out = pltpu.make_async_copy(lr, levels, out_sems.at[0])
            rows_out.start()
            rows_out.wait()
        else:
            for slot in range(BLOCKS):
                level_copy(slot).wait()
        out.wait()


PACK = (6, C, CL)
HU = 6
AHEAD = 3


def chain(plane, ending, place, packs, start, tau_own, tau_other, ck_own, ck_other, held=None):
    operands = [*packs, start, tau_own, tau_other, ck_own, ck_other] + ([] if plane == 0 else [held])
    return pl.pallas_call(
        functools.partial(chain_kernel, plane, ending),
        out_shape=[jax.ShapeDtypeStruct(ROWS if ending else TAU, F32), jax.ShapeDtypeStruct(PACK, BF16)],
        in_specs=[pl.BlockSpec(memory_space=pltpu.SMEM)] + [ANY] * len(operands),
        out_specs=[ANY, ANY],
        scratch_shapes=[
            pltpu.VMEM((HU * C, FL), F32),
            pltpu.VMEM(((HU + 2) * C, FL), BF16),
            pltpu.VMEM(((HU + 2) * C, FL), BF16),
            pltpu.VMEM((2 * BLOCKS, 3 * C, 3 * C), BF16),
            pltpu.VMEM((2 * BLOCKS, CU, C, CL), BF16),
            pltpu.VMEM((BLOCKS + 1, CU, C, CL), F32),
            pltpu.VMEM(ROWS, F32),
            pltpu.VMEM((3,) + PACK, BF16),
            pltpu.SemaphoreType.DMA((4 * BLOCKS + 3,)),
            pltpu.SemaphoreType.DMA((BLOCKS,)),
        ],
        input_output_aliases={} if plane == 0 else {9: 0},
        compiler_params=pltpu.CompilerParams(vmem_limit_bytes=VMEM_LIMIT),
        cost_estimate=pl.CostEstimate(
            flops=2 * 8 * 192 * 192 * CU * CL, bytes_accessed=6 << 20, transcendentals=8 * CU * C * CL
        ),
    )(place, *operands)


def final_kernel(sc, tile, edge, edge_swapped, recv, level, out):
    fresh, y, c = sc[0] == 0, sc[2], sc[3]
    pool, widen = pool_matrix(), widen_matrix()
    lane = lane_of((C, 128))

    def choose(here, a, b):
        return jnp.where(here, a.astype(F32), b.astype(F32)).astype(BF16)

    pairs = [4 * y + 2 * c + pair for pair in range(2)]
    parts = [part_of(pair, CU) for pair in pairs]
    firsts = [2 * (pair - CU * part) for pair, part in zip(pairs, parts)]
    for j in range(2 * BLOCKS):
        packed = jnp.zeros((C, 128), F32)
        for pair in range(2):
            first = firsts[pair]
            if j == 0:
                rows = [
                    choose(fresh, tile[first + r], recv[0, 2 * pair + r]) for r in range(2)
                ]
            else:
                h, i = (j - 1) // BLOCKS, (j - 1) % BLOCKS
                rows = [
                    choose(c == h, edge[i, 2 * pair + r], edge_swapped[i, 2 * pair + r]) for r in range(2)
                ]
            pooled = dot(rows[0], pool) + dot(rows[1], pool)
            if j == 0:
                goal = jnp.where(fresh, pooled, level[0, pair])
            else:
                goal = level[j, pair]
            for r, row in enumerate(corrected(rows[0], rows[1], goal, pooled, widen)):
                row = row.astype(F32)
                i = 2 * pair + r
                moved = pltpu.roll(row, (FL - 2 * EDGE + 32 * i - FP * parts[pair]) & (FL - 1), 1)[:, :128]
                packed = jnp.where((lane >= 32 * i) & (lane < 32 * i + 32), moved, packed)
        out[j] = packed.astype(BF16)


def final(place, tile, edge, edge_swapped, received, rows):
    return pl.pallas_call(
        final_kernel,
        out_shape=jax.ShapeDtypeStruct((2 * BLOCKS, C, 128), BF16),
        grid_spec=pltpu.PrefetchScalarGridSpec(
            num_scalar_prefetch=1,
            grid=(1,),
            in_specs=[
                whole(TILE),
                whole(EDGES),
                whole(EDGES),
                whole((1,) + EDGES[1:]),
                whole(ROWS),
            ],
            out_specs=whole((2 * BLOCKS, C, 128)),
        ),
        compiler_params=pltpu.CompilerParams(vmem_limit_bytes=VMEM_LIMIT),
    )(place, tile, edge, edge_swapped, received, rows)


def kernel_sources(i):
    pairs = []
    for z in range(ZS):
        for c in range(2):
            source = 4 * c + (z + i) % 4
            pairs.append((source * 2 + z // 4, z * 2 + c))
    return pairs


def per_device(image, weights):
    x, z, y, c = (lax.axis_index(name) for name in ("x", "z", "y", "c"))
    place = jnp.stack([x, z, y, c]).astype(jnp.int32)

    def swap(a):
        return lax.ppermute(a, "c", [(0, 1), (1, 0)])

    def hand_over(last):
        pairs = []
        for p in range(PLANES):
            pairs.append((2 * p, 2 * p + 1))
            if p + 1 < PLANES:
                pairs.append((2 * p + 1, 2 * p + 2))
        return lax.ppermute(last, ("x", "c"), pairs)

    def upward(pack, p):
        got = []
        for shift in (1, 0, -1):
            pairs = [
                (p * ZS + q, (p + 1) * ZS + q + shift) for q in range(ZS) if 0 <= q + shift < ZS
            ]
            got.append(lax.ppermute(pack, ("x", "z"), pairs))
        return got

    fetched = [lax.ppermute(weights, ("z", "c"), kernel_sources(i)) for i in range(BLOCKS)]
    wide = jnp.pad(image, ((0, 0), (0, 0), (2 * EDGE, 128)))
    piece = lax.dynamic_slice_in_dim(wide, 2 * OWN * z, FP, axis=2).reshape(C, 4 * FP)
    rows = lax.all_gather(piece, ("y", "c"))

    def all_levels(start, tau, kernels, kernels_other, last, edges):
        other = swap(tau)
        levels, received, swapped = None, None, None
        packs = [jnp.zeros(PACK, BF16)] * 3
        for p in range(PLANES):
            if p == PLANES - 1 and edges is not None:
                mine, others, *packs = lax.optimization_barrier((*edges, *packs))
                swapped = swap(others)
                rows = jnp.where(c == 1, mine[BLOCKS - 1 :], swapped[BLOCKS - 1 :])
                received = lax.ppermute(rows, "x", [(q, q + 1) for q in range(PLANES - 1)])
            levels, pack = chain(
                p, edges is not None, place, packs, start, tau, other, kernels, kernels_other, levels
            )
            if p == 0 and edges is None:
                pack, last = lax.optimization_barrier((pack, last))
            if p + 1 < PLANES:
                packs = upward(pack, p)
            if p == 0 and edges is None:
                received = hand_over(last)
        return levels, swapped, received

    tau, ends, wk, ck, last, tile, start = first_sweeps(place, fetched, rows)
    ck_other = swap(ck)
    levels, _, received = all_levels(start, tau, ck, ck_other, last, None)

    before = ends.at[0].set(jnp.where((x == 0) & (c == 0), tile, received.reshape(TILE)))
    tau, edge, edge_other = later_sweeps(place, wk, ck, before, levels)
    levels, swapped, received = all_levels(start, tau, ck, ck_other, None, (edge, edge_other))

    parts = final(place, tile, edge, swapped, received, levels)
    got = lax.all_to_all(parts, "z", 0, 0, tiled=True)
    return got.reshape(ZS, C, 4, 2 * OWN).transpose(1, 2, 0, 3).reshape(1, C, 4, WIDTH)


def solution(mesh):
    split = Mesh(mesh.devices.reshape(PLANES, ZS, YS, 2), ("x", "z", "y", "c"))
    return jax.shard_map(
        per_device,
        mesh=split,
        in_specs=(P(None, ("y", "c"), None), P(("x", "z"), None, None)),
        out_specs=P(("x", "z"), None, ("y", "c"), None),
        check_vma=False,
    )
```

time: 1250 us -> 236 us (0.19)
  the two profiles are of different devices: /device:TPU:38 before, /device:TPU:6 now
where the time goes in v1:
time: 236 us; the launch traced here: 235 us
  Pallas kernels  73.9 us (31%)
  waiting for transfers between devices  54.5 us (23%)
  blocking collectives  49.2 us (21%)
  starting transfers between devices  44.2 us (19%)
  local copies, waits for them, and re-layouts  9.83 us (4%)
  other arithmetic  2.8 us (1%)
    ppermute x18, waiting for transfers between devices, upward(): got.append(lax.ppermute(pack, ('x', 'z'), pairs))  48.8 us
    all_gather x1, blocking collectives, per_device(): rows = lax.all_gather(piece, ('y', 'c'))  28.5 us
    pallas_call x1, Pallas kernels, first_sweeps(): pl.pallas_call(first_kernel, out_shape=[jax.ShapeDtypeStruct(TAU, BF16),...  25.5 us
    pallas_call x1, Pallas kernels, later_sweeps(): pl.pallas_call(later_kernel, out_shape=[jax.ShapeDtypeStruct(TAU, BF16),...  25 us
    all_to_all x1, blocking collectives, per_device(): got = lax.all_to_all(parts, 'z', 0, 0, tiled=True)  20.6 us
    pallas_call x8, Pallas kernels, chain(): pl.pallas_call(functools.partial(chain_kernel, plane, ending), out_shape=...  19.5 us
    ppermute x18, starting transfers between devices, upward(): got.append(lax.ppermute(pack, ('x', 'z'), pairs))  14.5 us
    ppermute x4, starting transfers between devices, per_device(): lax.ppermute(weights, ('z', 'c'), kernel_sources(i))  13.9 us
  transfers between devices with their start and end apart: 28, of which 5 were waited for; matrix products, arithmetic and copies ran while one was open for 1% of the time, Pallas kernels for 7%

profile of v1, /device:TPU:6, one launch (start us, length us, event | category | flops | bytes accessed | tf_op | source)
XLA Modules:
  0.0 235.1 jit_solution(17838671123867868395)
XLA Ops:
  0.0 7.9 %collective-permute-start.1 = (bf16[4,64,576]{2,1,0:T(8,128)(2,1)}, bf16[4,64,576]{2,1,0:T(8,128)(2,1)S(1)}, u32[]{:S(2)}, u32[]{:S(2)}) collective-permute-start(bf16[4,64,576]{2,1,0:T(8,128)(2,1)} %param.5), channel_id=1, source_target_pairs={{16,0},{80,1},{32,16},{96,17},{48,32},{112,33},{0,48},{64,49},{17,... | collective-permute-start | bytes 884744 | tf_op jit(solution)/shard_map/ppermute | solution.py:595
  7.9 1.6 collective-permute-start
  9.5 1.9 collective-permute-start.3
  11.4 2.5 %collective-permute-start.2 = (bf16[4,64,576]{2,1,0:T(8,128)(2,1)}, bf16[4,64,576]{2,1,0:T(8,128)(2,1)S(1)}, u32[]{:S(2)}, u32[]{:S(2)}) collective-permute-start(bf16[4,64,576]{2,1,0:T(8,128)(2,1)} %param.5), channel_id=1, source_target_pairs={{32,0},{96,1},{48,16},{112,17},{0,32},{64,33},{16,48},{80,49},{33,... | collective-permute-start | bytes 884744 | tf_op jit(solution)/shard_map/ppermute | solution.py:595
  13.9 1.1 pad_dynamic-slice_fusion
  15.7 28.5 %all_gather.3.source = bf16[16,64,320]{2,1,0:T(8,128)(2,1)} all-gather(bf16[1,64,320]{2,1,0:T(8,128)(2,1)S(1)} %all_gather_reshape.3), channel_id=1, replica_groups=mesh['x'=4,'z'=8,'y'=8,'c'=2] {'y','c'}, dimensions={0}, use_global_device_ids=true | all-gather | bytes 696320 | tf_op jit(solution)/shard_map/all_gather | solution.py:598
  44.3 0.7 copy-done.26
  45.2 0.7 copy-done.29
  46.0 25.5 %shard_map.28 = (bf16[4,11,64,128]{3,2,1,0:T(8,128)(2,1)}, bf16[5,22,64,256]{3,2,1,0:T(8,128)(2,1)}, bf16[4,4,192,192]{3,2,1,0:T(8,128)(2,1)}, bf16[4,192,192]{2...) custom-call(s32[4]{0:T(128)} %pad_add_fusion.sc, ...), custom_call_target="tpu_custom_call" | custom-call | flops 6643777536 | bytes 16777216 | tf_op jit(solution)/shard_map/pallas_call | solution.py:279
  71.4 2.3 collective-permute-start.4
  73.7 2.1 collective-permute-start.5
  75.8 1.8 collective-permute-done.5.ck_other
  78.6 0.9 shard_map.29
  79.5 2.1 collective-permute-start.6
  81.5 0.7 collective-permute-start.9
  82.2 0.7 collective-permute-start.8
  82.9 0.7 collective-permute-start.7
  84.3 0.9 shard_map.30
  85.2 0.7 collective-permute-start.12
  85.9 0.7 collective-permute-start.11
  86.5 0.7 collective-permute-start.10
  87.9 0.9 shard_map.31
  88.8 1.3 collective-permute-start.15
  90.1 1.3 collective-permute-start.14
  91.4 0.7 collective-permute-start.13
  92.1 31.9 %collective-permute-done.15.above = bf16[6,64,128]{2,1,0:T(8,128)(2,1)S(1)} collective-permute-done((bf16[6,64,128]{2,1,0:T(8,128)(2,1)}, bf16[6,64,128]{2,1,0:T(8,128)(2,1)S(1)}, u32[]{:S(2)}, u32[]{:S(2)}) %collective-permute-start.15) | collective-permute-done | bytes 98336 | tf_op jit(solution)/shard_map/ppermute | solution.py:592
  124.7 7.1 %shard_map.32 = (f32[4,11,64,128]{3,2,1,0:T(8,128)}, bf16[6,64,128]{2,1,0:T(8,128)(2,1)}) custom-call(s32[4]{0:T(128)} %pad_add_fusion.sc, bf16[6,64,128]{2,1,0:T(8,128)(2,1)} %copy-done.17, bf16[6,64,128]{2,1,0:T(8,128)(2,1)} %copy-done.16, bf16[6,64,128]{2,1,0:T(8,128)(2,1)} %copy-done.15, ...), custom_call_target="tpu_custom_call", output_to_operand_aliasing={{0}: (9, {})} | custom-call | flops 830472192 | bytes 6291456 | tf_op jit(solution)/shard_map/pallas_call | solution.py:480
  131.8 1.2 bitcast_dynamic-update-slice_fusion.before
  133.0 25.0 %shard_map.33 = (bf16[4,11,64,128]{3,2,1,0:T(8,128)(2,1)}, bf16[4,4,64,256]{3,2,1,0:T(8,128)(2,1)}, bf16[4,4,64,256]{3,2,1,0:T(8,128)(2,1)}) custom-call(s32[4]{0:T(128)} %pad_add_fusion.sc, bf16[4,4,192,192]{3,2,1,0:T(8,128)(2,1)} %get-tuple-element.49.wk, bf16[4,192,192]{2,1,0:T(8,128)(2,1)} %get-tuple-element.50.ck_own.ck, ...), custom_call_target="tpu_custom_call" | custom-call | flops 6643777536 | bytes 16777216 | tf_op jit(solution)/shard_map/pallas_call | solution.py:311
  158.0 6.2 %collective-permute-start.16 = (bf16[4,11,64,128]{3,2,1,0:T(8,128)(2,1)}, bf16[4,11,64,128]{3,2,1,0:T(8,128)(2,1)S(1)}, u32[]{:S(2)}, u32[]{:S(2)}) collective-permute-start(bf16[4,11,64,128]{3,2,1,0:T(8,128)(2,1)} %get-tuple-element.66.tau_own), channel_id=1, source_target_pairs={{0,1},{1,0},{2,3},{3,2},{4,5},{5,4},{6,7},{7,6},{8,9},{9,8},{10,11... | collective-permute-start | bytes 2162696 | tf_op jit(solution)/shard_map/ppermute | solution.py:576
  164.2 2.0 collective-permute-done.16.tau_other
  166.2 0.9 copy-done.2
  167.1 0.9 shard_map.34
  169.3 0.7 collective-permute-start.17
  170.7 0.9 shard_map.35
  174.3 1.0 shard_map.36
  175.3 1.3 collective-permute-start.25
  176.6 1.3 collective-permute-start.24
  177.9 0.7 collective-permute-start.23
  178.6 16.9 %collective-permute-done.25.above = bf16[6,64,128]{2,1,0:T(8,128)(2,1)S(1)} collective-permute-done((bf16[6,64,128]{2,1,0:T(8,128)(2,1)}, bf16[6,64,128]{2,1,0:T(8,128)(2,1)S(1)}, u32[]{:S(2)}, u32[]{:S(2)}) %collective-permute-start.25) | collective-permute-done | bytes 98336 | tf_op jit(solution)/shard_map/ppermute | solution.py:592
  195.5 1.9 collective-permute-start.26
  197.5 1.9 collective-permute-done.26.edge_swapped
  199.3 1.0 slice_select_fusion
  200.4 1.3 collective-permute-start.27
  201.7 7.0 %shard_map.37 = (f32[8,2,64,128]{3,2,1,0:T(8,128)}, bf16[6,64,128]{2,1,0:T(8,128)(2,1)}) custom-call(s32[4]{0:T(128)} %pad_add_fusion.sc, bf16[6,64,128]{2,1,0:T(8,128)(2,1)} %copy-done.8, bf16[6,64,128]{2,1,0:T(8,128)(2,1)} %copy-done.7, bf16[6,64,128]{2,1,0:T(8,128)(2,1)} %copy-done.6, ...), custom_call_target="tpu_custom_call", output_to_operand_aliasing={{0}: (9, {})} | custom-call | flops 830472192 | bytes 6291456 | tf_op jit(solution)/shard_map/pallas_call | solution.py:480
  209.5 4.0 %shard_map.38 = bf16[8,64,128]{2,1,0:T(8,128)(2,1)} custom-call(s32[4]{0:T(128)} %pad_add_fusion.sc, bf16[22,64,256]{2,1,0:T(8,128)(2,1)} %get-tuple-element.48.tile, bf16[4,4,64,256]{3,2,1,0:T(8,128)(2,1)} %get-tuple-element.73.edge, bf16[4,4,64,256]{3,2,1,0:T(8,128)(2,1)} %copy-done.4, bf16[1,4,64,256]{3,2,1,0:T(8,128)(2,1)} %copy-done.5, ...), custom_call_target="tpu_custom_call" | custom-call | tf_op jit(solution)/shard_map/pallas_call | solution.py:543
  213.5 20.6 %all_to_all.5 = bf16[8,64,128]{2,1,0:T(8,128)(2,1)S(1)} all-to-all(bf16[8,64,128]{2,1,0:T(8,128)(2,1)} %shard_map.38), channel_id=1, replica_groups=mesh['x'=4,'z'=8,'y'=8,'c'=2] {'z'}, dimensions={0} | all-to-all | bytes 262144 | tf_op jit(solution)/shard_map/all_to_all | solution.py:630
  234.3 0.8 copy.15
  (90 shorter events, 9.7 us)
Async XLA Ops:
  0.0 44.3 %collective-permute-start.1 = (bf16[4,64,576]{2,1,0:T(8,128)(2,1)}, bf16[4,64,576]{2,1,0:T(8,128)(2,1)S(1)}, u32[]{:S(2)}, u32[]{:S(2)}) collective-permute-start(bf16[4,64,576]{2,1,0:T(8,128)(2,1)} %param.5), channel_id=1, source_target_pairs={{16,0},{80,1},{32,16},{96,17},{48,32},{112,33},{0,48},{64,49},{17,... | collective-permute-start | bytes 884744 | tf_op jit(solution)/shard_map/ppermute | solution.py:595
  7.9 36.4 %collective-permute-start = (bf16[4,64,576]{2,1,0:T(8,128)(2,1)}, bf16[4,64,576]{2,1,0:T(8,128)(2,1)S(1)}, u32[]{:S(2)}, u32[]{:S(2)}) collective-permute-start(bf16[4,64,576]{2,1,0:T(8,128)(2,1)} %param.5), channel_id=1, source_target_pairs={{0,0},{64,1},{16,16},{80,17},{32,32},{96,33},{48,48},{112,49},{1,6... | collective-permute-start | bytes 884744 | tf_op jit(solution)/shard_map/ppermute | solution.py:595
  9.5 34.7 %collective-permute-start.3 = (bf16[4,64,576]{2,1,0:T(8,128)(2,1)}, bf16[4,64,576]{2,1,0:T(8,128)(2,1)S(1)}, u32[]{:S(2)}, u32[]{:S(2)}) collective-permute-start(bf16[4,64,576]{2,1,0:T(8,128)(2,1)} %param.5), channel_id=1, source_target_pairs={{48,0},{112,1},{0,16},{64,17},{16,32},{80,33},{32,48},{96,49},{49,... | collective-permute-start | bytes 884744 | tf_op jit(solution)/shard_map/ppermute | solution.py:595
  11.4 32.9 %collective-permute-start.2 = (bf16[4,64,576]{2,1,0:T(8,128)(2,1)}, bf16[4,64,576]{2,1,0:T(8,128)(2,1)S(1)}, u32[]{:S(2)}, u32[]{:S(2)}) collective-permute-start(bf16[4,64,576]{2,1,0:T(8,128)(2,1)} %param.5), channel_id=1, source_target_pairs={{32,0},{96,1},{48,16},{112,17},{0,32},{64,33},{16,48},{80,49},{33,... | collective-permute-start | bytes 884744 | tf_op jit(solution)/shard_map/ppermute | solution.py:595
  44.3 0.8 copy-start.26
  44.3 0.9 copy-start.27
  44.3 1.0 copy-start.28
  45.2 0.7 copy-start.29
  71.4 6.1 %collective-permute-start.4 = (bf16[4,11,64,128]{3,2,1,0:T(8,128)(2,1)}, bf16[4,11,64,128]{3,2,1,0:T(8,128)(2,1)S(1)}, u32[]{:S(2)}, u32[]{:S(2)}) collective-permute-start(bf16[4,11,64,128]{3,2,1,0:T(8,128)(2,1)} %get-tuple-element.53.tau_own), channel_id=1, source_target_pairs={{0,1},{1,0},{2,3},{3,2},{4,5},{5,4},{6,7},{7,6},{8,9},{9,8},{10,11... | collective-permute-start | bytes 2162696 | tf_op jit(solution)/shard_map/ppermute | solution.py:576
  73.7 3.8 %collective-permute-start.5 = (bf16[4,192,192]{2,1,0:T(8,128)(2,1)}, bf16[4,192,192]{2,1,0:T(8,128)(2,1)S(1)}, u32[]{:S(2)}, u32[]{:S(2)}) collective-permute-start(bf16[4,192,192]{2,1,0:T(8,128)(2,1)} %get-tuple-element.50.ck_own.ck), channel_id=1, source_target_pairs={{0,1},{1,0},{2,3},{3,2},{4,5},{5,4},{6,7},{7,6},{8,9},{9,8},{10,11... | collective-permute-start | bytes 884744 | tf_op jit(solution)/shard_map/ppermute | solution.py:576
  77.5 0.8 copy-start
  77.5 1.1 copy-start.1
  77.5 1.9 copy-start.24
  79.5 52.3 %collective-permute-start.6 = (bf16[1408,256]{1,0:T(8,128)(2,1)S(1)}, bf16[1408,256]{1,0:T(8,128)(2,1)S(1)}, u32[]{:S(2)}, u32[]{:S(2)}) collective-permute-start(bf16[1408,256]{1,0:T(8,128)(2,1)S(1)} %copy-done.24), channel_id=1, source_target_pairs={{0,1},{1,128},{128,129},{129,256},{256,257},{257,384},{384,385},{2... | collective-permute-start | bytes 2162696 | tf_op jit(solution)/shard_map/ppermute | solution.py:584
  81.5 2.0 collective-permute-start.9
  82.2 1.4 collective-permute-start.8
  82.9 0.7 collective-permute-start.7
  83.6 0.7 copy-start.22
  85.2 2.0 collective-permute-start.12
  85.9 1.4 collective-permute-start.11
  86.5 0.7 collective-permute-start.10
  87.3 0.7 copy-start.23
  88.8 35.2 %collective-permute-start.15 = (bf16[6,64,128]{2,1,0:T(8,128)(2,1)}, bf16[6,64,128]{2,1,0:T(8,128)(2,1)S(1)}, u32[]{:S(2)}, u32[]{:S(2)}) collective-permute-start(bf16[6,64,128]{2,1,0:T(8,128)(2,1)} %get-tuple-element.61), channel_id=1, source_target_pairs={{272,384},{288,400},{304,416},{320,432},{336,448},{352,464},{368,4... | collective-permute-start | bytes 294920 | tf_op jit(solution)/shard_map/ppermute | solution.py:592
  90.1 33.9 %collective-permute-start.14 = (bf16[6,64,128]{2,1,0:T(8,128)(2,1)}, bf16[6,64,128]{2,1,0:T(8,128)(2,1)S(1)}, u32[]{:S(2)}, u32[]{:S(2)}) collective-permute-start(bf16[6,64,128]{2,1,0:T(8,128)(2,1)} %get-tuple-element.61), channel_id=1, source_target_pairs={{256,384},{272,400},{288,416},{304,432},{320,448},{336,464},{352,4... | collective-permute-start | bytes 294920 | tf_op jit(solution)/shard_map/ppermute | solution.py:592
  91.4 32.6 %collective-permute-start.13 = (bf16[6,64,128]{2,1,0:T(8,128)(2,1)}, bf16[6,64,128]{2,1,0:T(8,128)(2,1)S(1)}, u32[]{:S(2)}, u32[]{:S(2)}) collective-permute-start(bf16[6,64,128]{2,1,0:T(8,128)(2,1)} %get-tuple-element.61), channel_id=1, source_target_pairs={{256,400},{272,416},{288,432},{304,448},{320,464},{336,480},{352,4... | collective-permute-start | bytes 294920 | tf_op jit(solution)/shard_map/ppermute | solution.py:592
  124.0 0.7 copy-start.16
  124.0 0.7 copy-start.17
  124.7 7.1 %copy-start.3 = (bf16[22,64,256]{2,1,0:T(8,128)(2,1)S(1)}, bf16[22,64,256]{2,1,0:T(8,128)(2,1)}, u32[]{:S(2)}) copy-start(bf16[22,64,256]{2,1,0:T(8,128)(2,1)} %get-tuple-element.48.tile) | copy-start | bytes 2162692
  158.0 8.2 %collective-permute-start.16 = (bf16[4,11,64,128]{3,2,1,0:T(8,128)(2,1)}, bf16[4,11,64,128]{3,2,1,0:T(8,128)(2,1)S(1)}, u32[]{:S(2)}, u32[]{:S(2)}) collective-permute-start(bf16[4,11,64,128]{3,2,1,0:T(8,128)(2,1)} %get-tuple-element.66.tau_own), channel_id=1, source_target_pairs={{0,1},{1,0},{2,3},{3,2},{4,5},{5,4},{6,7},{7,6},{8,9},{9,8},{10,11... | collective-permute-start | bytes 2162696 | tf_op jit(solution)/shard_map/ppermute | solution.py:576
  166.2 0.9 copy-start.2
  168.0 2.0 collective-permute-start.19
  168.6 1.4 collective-permute-start.18
  169.3 0.7 collective-permute-start.17
  170.0 0.7 copy-start.13
  171.6 2.0 collective-permute-start.22
  172.3 1.4 collective-permute-start.21
  172.9 0.7 collective-permute-start.20
  173.7 0.7 copy-start.14
  174.3 21.2 %copy-start.25 = (bf16[4,4,64,256]{3,2,1,0:T(8,128)(2,1)S(1)}, bf16[4,4,64,256]{3,2,1,0:T(8,128)(2,1)}, u32[]{:S(2)}) copy-start(bf16[4,4,64,256]{3,2,1,0:T(8,128)(2,1)} %get-tuple-element.72) | copy-start | bytes 1572868
  175.3 20.2 %collective-permute-start.25 = (bf16[6,64,128]{2,1,0:T(8,128)(2,1)}, bf16[6,64,128]{2,1,0:T(8,128)(2,1)S(1)}, u32[]{:S(2)}, u32[]{:S(2)}) collective-permute-start(bf16[6,64,128]{2,1,0:T(8,128)(2,1)} %get-tuple-element.71), channel_id=1, source_target_pairs={{272,384},{288,400},{304,416},{320,432},{336,448},{352,464},{368,4... | collective-permute-start | bytes 294920 | tf_op jit(solution)/shard_map/ppermute | solution.py:592
  176.6 18.9 %collective-permute-start.24 = (bf16[6,64,128]{2,1,0:T(8,128)(2,1)}, bf16[6,64,128]{2,1,0:T(8,128)(2,1)S(1)}, u32[]{:S(2)}, u32[]{:S(2)}) collective-permute-start(bf16[6,64,128]{2,1,0:T(8,128)(2,1)} %get-tuple-element.71), channel_id=1, source_target_pairs={{256,384},{272,400},{288,416},{304,432},{320,448},{336,464},{352,4... | collective-permute-start | bytes 294920 | tf_op jit(solution)/shard_map/ppermute | solution.py:592
  177.9 17.6 %collective-permute-start.23 = (bf16[6,64,128]{2,1,0:T(8,128)(2,1)}, bf16[6,64,128]{2,1,0:T(8,128)(2,1)S(1)}, u32[]{:S(2)}, u32[]{:S(2)}) collective-permute-start(bf16[6,64,128]{2,1,0:T(8,128)(2,1)} %get-tuple-element.71), channel_id=1, source_target_pairs={{256,400},{272,416},{288,432},{304,448},{320,464},{336,480},{352,4... | collective-permute-start | bytes 294920 | tf_op jit(solution)/shard_map/ppermute | solution.py:592
  195.5 6.2 %copy-start.6 = (bf16[6,64,128]{2,1,0:T(8,128)(2,1)}, bf16[6,64,128]{2,1,0:T(8,128)(2,1)S(1)}, u32[]{:S(2)}) copy-start(bf16[6,64,128]{2,1,0:T(8,128)(2,1)S(1)} %collective-permute-done.25.above) | copy-start | bytes 294916
  195.5 6.2 %copy-start.7 = (bf16[6,64,128]{2,1,0:T(8,128)(2,1)}, bf16[6,64,128]{2,1,0:T(8,128)(2,1)S(1)}, u32[]{:S(2)}) copy-start(bf16[6,64,128]{2,1,0:T(8,128)(2,1)S(1)} %collective-permute-done.24.same) | copy-start | bytes 294916
  195.5 6.2 %copy-start.8 = (bf16[6,64,128]{2,1,0:T(8,128)(2,1)}, bf16[6,64,128]{2,1,0:T(8,128)(2,1)S(1)}, u32[]{:S(2)}) copy-start(bf16[6,64,128]{2,1,0:T(8,128)(2,1)S(1)} %collective-permute-done.23.below) | copy-start | bytes 294916
  195.5 3.8 %collective-permute-start.26 = (bf16[4,4,64,256]{3,2,1,0:T(8,128)(2,1)S(1)}, bf16[4,4,64,256]{3,2,1,0:T(8,128)(2,1)S(1)}, u32[]{:S(2)}, u32[]{:S(2)}) collective-permute-start(bf16[4,4,64,256]{3,2,1,0:T(8,128)(2,1)S(1)} %copy-done.25), channel_id=1, source_target_pairs={{0,1},{1,0},{2,3},{3,2},{4,5},{5,4},{6,7},{7,6},{8,9},{9,8},{10,11... | collective-permute-start | bytes 1572872 | tf_op jit(solution)/shard_map/ppermute | solution.py:576
  199.3 9.4 %copy-start.4 = (bf16[4,4,64,256]{3,2,1,0:T(8,128)(2,1)}, bf16[4,4,64,256]{3,2,1,0:T(8,128)(2,1)S(1)}, u32[]{:S(2)}) copy-start(bf16[4,4,64,256]{3,2,1,0:T(8,128)(2,1)S(1)} %collective-permute-done.26.edge_swapped) | copy-start | bytes 1572868
  200.4 8.4 %collective-permute-start.27 = (bf16[1,4,64,256]{3,2,1,0:T(8,128)(2,1)S(1)}, bf16[1,4,64,256]{3,2,1,0:T(8,128)(2,1)S(1)}, u32[]{:S(2)}, u32[]{:S(2)}) collective-permute-start(bf16[1,4,64,256]{3,2,1,0:T(8,128)(2,1)S(1)} %slice_select_fusion), channel_id=1, source_target_pairs={{0,128},{128,256},{256,384},{1,129},{129,257},{257,385},{2,130},{1... | collective-permute-start | bytes 393224 | tf_op jit(solution)/shard_map/ppermute | solution.py:609
  (10 other events, 6.4 us)

commit v2 on v1

--- a/solution.py
+++ b/solution.py
@@ -163,10 +163,10 @@
             dst[unit(u + 1), :] = (x + mf[u >= FU - 2] * jnp.tanh(conv)).astype(BF16)
         fine_halo(dst)
 
-    @pl.loop(0, 2)
-    def _(t):
-        layer(2 * t, xa, xb)
-        layer(2 * t + 1, xb, xa)
+    layer(0, xa, xb)
+    layer(1, xb, xa)
+    layer(2, xa, xb)
+    layer(3, xb, xa)
 
 
 def write_tau(ck, xa, sp, sb, tau_out, pool, mc):
@@ -599,7 +599,8 @@
 
     def all_levels(start, tau, kernels, kernels_other, last, edges):
         other = swap(tau)
-        levels, received, swapped = None, None, None
+        levels, swapped = None, None
+        received = hand_over(last) if edges is None else None
         packs = [jnp.zeros(PACK, BF16)] * 3
         for p in range(PLANES):
             if p == PLANES - 1 and edges is not None:
@@ -610,12 +611,8 @@
             levels, pack = chain(
                 p, edges is not None, place, packs, start, tau, other, kernels, kernels_other, levels
             )
-            if p == 0 and edges is None:
-                pack, last = lax.optimization_barrier((pack, last))
             if p + 1 < PLANES:
                 packs = upward(pack, p)
-            if p == 0 and edges is None:
-                received = hand_over(last)
         return levels, swapped, received
 
     tau, ends, wk, ck, last, tile, start = first_sweeps(place, fetched, rows)

time: 236 us -> 226 us (0.958)
  Pallas kernels: 73.9 us -> 67.3 us
  starting transfers between devices: 44.2 us -> 40.1 us
  waiting for transfers between devices: 54.5 us -> 57.9 us
  blocking collectives: 49.2 us -> 46.2 us
    ppermute x18, waiting for transfers between devices: 48.8 us -> 53.7 us  [upward(): got.append(lax.ppermute(pack, ('x', 'z'), pairs))]
    ppermute x4, starting transfers between devices: 12.4 us -> 8.14 us  [swap(): return lax.ppermute(a, 'c', [(0, 1), (1, 0)])]
    pallas_call x1, Pallas kernels: 25 us -> 21.2 us  [later_sweeps(): pl.pallas_call(later_kernel, out_shape=[jax.ShapeDtypeStruct(TAU, BF16),...]
    pallas_call x1, Pallas kernels: 25.5 us -> 22.6 us  [first_sweeps(): pl.pallas_call(first_kernel, out_shape=[jax.ShapeDtypeStruct(TAU, BF16),...]
    all_to_all x1, blocking collectives: 20.6 us -> 17.8 us  [per_device(): got = lax.all_to_all(parts, 'z', 0, 0, tiled=True)]
    unnamed x60 -> x58, local copies, waits for them, and re-layouts: 7.01 us -> 6.76 us
  transfers between devices with their start and end apart: 28 -> 28, of which waited for: 5 -> 6; matrix products, arithmetic and copies ran while one was open for 1% -> 2% of each run, Pallas kernels for 7% -> 4%
where the time goes in v2:
time: 226 us; the launch traced here: 225 us
  Pallas kernels  67.3 us (30%)
  waiting for transfers between devices  57.9 us (26%)
  blocking collectives  46.2 us (20%)
  starting transfers between devices  40.1 us (18%)
  local copies, waits for them, and re-layouts  9.67 us (4%)
  other arithmetic  2.81 us (1%)
    ppermute x18, waiting for transfers between devices, upward(): got.append(lax.ppermute(pack, ('x', 'z'), pairs))  53.7 us
    all_gather x1, blocking collectives, per_device(): rows = lax.all_gather(piece, ('y', 'c'))  28.4 us
    pallas_call x1, Pallas kernels, first_sweeps(): pl.pallas_call(first_kernel, out_shape=[jax.ShapeDtypeStruct(TAU, BF16),...  22.6 us
    pallas_call x1, Pallas kernels, later_sweeps(): pl.pallas_call(later_kernel, out_shape=[jax.ShapeDtypeStruct(TAU, BF16),...  21.2 us
    pallas_call x8, Pallas kernels, chain(): pl.pallas_call(functools.partial(chain_kernel, plane, ending), out_shape=...  19.5 us
    all_to_all x1, blocking collectives, per_device(): got = lax.all_to_all(parts, 'z', 0, 0, tiled=True)  17.8 us
    ppermute x18, starting transfers between devices, upward(): got.append(lax.ppermute(pack, ('x', 'z'), pairs))  14.5 us
    ppermute x4, starting transfers between devices, per_device(): lax.ppermute(weights, ('z', 'c'), kernel_sources(i))  13.9 us
  transfers between devices with their start and end apart: 28, of which 6 were waited for; matrix products, arithmetic and copies ran while one was open for 2% of the time, Pallas kernels for 4%

profile of v2, /device:TPU:6, one launch (start us, length us, event | category | flops | bytes accessed | tf_op | source)
XLA Modules:
  0.0 224.7 jit_solution(14868082532673779522)
XLA Ops:
  0.0 1.6 collective-permute-start
  1.6 7.9 %collective-permute-start.1 = (bf16[4,64,576]{2,1,0:T(8,128)(2,1)}, bf16[4,64,576]{2,1,0:T(8,128)(2,1)S(1)}, u32[]{:S(2)}, u32[]{:S(2)}) collective-permute-start(bf16[4,64,576]{2,1,0:T(8,128)(2,1)} %param.5), channel_id=1, source_target_pairs={{16,0},{80,1},{32,16},{96,17},{48,32},{112,33},{0,48},{64,49},{17,... | collective-permute-start | bytes 884744 | tf_op jit(solution)/shard_map/ppermute | solution.py:595
  9.5 1.9 collective-permute-start.2
  11.4 2.5 %collective-permute-start.3 = (bf16[4,64,576]{2,1,0:T(8,128)(2,1)}, bf16[4,64,576]{2,1,0:T(8,128)(2,1)S(1)}, u32[]{:S(2)}, u32[]{:S(2)}) collective-permute-start(bf16[4,64,576]{2,1,0:T(8,128)(2,1)} %param.5), channel_id=1, source_target_pairs={{48,0},{112,1},{0,16},{64,17},{16,32},{80,33},{32,48},{96,49},{49,... | collective-permute-start | bytes 884744 | tf_op jit(solution)/shard_map/ppermute | solution.py:595
  13.9 1.1 pad_dynamic-slice_fusion
  15.7 28.4 %all_gather.3.source = bf16[16,64,320]{2,1,0:T(8,128)(2,1)} all-gather(bf16[1,64,320]{2,1,0:T(8,128)(2,1)S(1)} %all_gather_reshape.3), channel_id=1, replica_groups=mesh['x'=4,'z'=8,'y'=8,'c'=2] {'y','c'}, dimensions={0}, use_global_device_ids=true | all-gather | bytes 696320 | tf_op jit(solution)/shard_map/all_gather | solution.py:598
  44.2 0.7 copy-done.25
  45.1 0.7 copy-done.28
  45.8 22.6 %shard_map.28 = (bf16[4,11,64,128]{3,2,1,0:T(8,128)(2,1)}, bf16[5,22,64,256]{3,2,1,0:T(8,128)(2,1)}, bf16[4,4,192,192]{3,2,1,0:T(8,128)(2,1)}, bf16[4,192,192]{2...) custom-call(s32[4]{0:T(128)} %pad_add_fusion.sc, ...), custom_call_target="tpu_custom_call" | custom-call | flops 6643777536 | bytes 16777216 | tf_op jit(solution)/shard_map/pallas_call | solution.py:279
  68.4 2.3 %collective-permute-start.5 = (bf16[4,11,64,128]{3,2,1,0:T(8,128)(2,1)}, bf16[4,11,64,128]{3,2,1,0:T(8,128)(2,1)S(1)}, u32[]{:S(2)}, u32[]{:S(2)}) collective-permute-start(bf16[4,11,64,128]{3,2,1,0:T(8,128)(2,1)} %get-tuple-element.52.tau_own), channel_id=1, source_target_pairs={{0,1},{1,0},{2,3},{3,2},{4,5},{5,4},{6,7},{7,6},{8,9},{9,8},{10,11... | collective-permute-start | bytes 2162696 | tf_op jit(solution)/shard_map/ppermute | solution.py:576
  70.7 2.1 collective-permute-start.6
  72.7 2.3 %collective-permute-start.4 = (bf16[1408,256]{1,0:T(8,128)(2,1)}, bf16[1408,256]{1,0:T(8,128)(2,1)S(1)}, u32[]{:S(2)}, u32[]{:S(2)}) collective-permute-start(bf16[1408,256]{1,0:T(8,128)(2,1)} %get-tuple-element.50), channel_id=1, source_target_pairs={{0,1},{1,128},{128,129},{129,256},{256,257},{257,384},{384,385},{2... | collective-permute-start | bytes 2162696 | tf_op jit(solution)/shard_map/ppermute | solution.py:584
  75.0 0.8 broadcast_1_below_same_above.2.below.same.above
  76.0 0.9 shard_map.29
  76.9 0.7 collective-permute-start.7
  77.6 0.7 collective-permute-start.8
  78.3 0.7 collective-permute-start.9
  79.7 0.9 shard_map.30
  80.6 0.7 collective-permute-start.10
  81.2 0.7 collective-permute-start.11
  81.9 0.7 collective-permute-start.12
  83.3 1.0 shard_map.31
  84.3 0.7 collective-permute-start.13
  85.0 1.3 collective-permute-start.14
  86.3 1.3 collective-permute-start.15
  87.6 1.2 bitcast_dynamic-update-slice_fusion.before
  88.8 33.9 %collective-permute-done.14.same = bf16[6,64,128]{2,1,0:T(8,128)(2,1)S(1)} collective-permute-done((bf16[6,64,128]{2,1,0:T(8,128)(2,1)}, bf16[6,64,128]{2,1,0:T(8,128)(2,1)S(1)}, u32[]{:S(2)}, u32[]{:S(2)}) %collective-permute-start.14) | collective-permute-done | bytes 98336 | tf_op jit(solution)/shard_map/ppermute | solution.py:592
  122.7 2.1 collective-permute-done.15.above
  125.5 6.9 %shard_map.32 = (f32[4,11,64,128]{3,2,1,0:T(8,128)}, bf16[6,64,128]{2,1,0:T(8,128)(2,1)}) custom-call(s32[4]{0:T(128)} %pad_add_fusion.sc, bf16[6,64,128]{2,1,0:T(8,128)(2,1)} %copy-done.15, bf16[6,64,128]{2,1,0:T(8,128)(2,1)} %copy-done.17, bf16[6,64,128]{2,1,0:T(8,128)(2,1)} %copy-done.19, ...), custom_call_target="tpu_custom_call", output_to_operand_aliasing={{0}: (9, {})} | custom-call | flops 830472192 | bytes 6291456 | tf_op jit(solution)/shard_map/pallas_call | solution.py:480
  132.4 21.2 %shard_map.33 = (bf16[4,11,64,128]{3,2,1,0:T(8,128)(2,1)}, bf16[4,4,64,256]{3,2,1,0:T(8,128)(2,1)}, bf16[4,4,64,256]{3,2,1,0:T(8,128)(2,1)}) custom-call(s32[4]{0:T(128)} %pad_add_fusion.sc, bf16[4,4,192,192]{3,2,1,0:T(8,128)(2,1)} %get-tuple-element.47.wk, bf16[4,192,192]{2,1,0:T(8,128)(2,1)} %get-tuple-element.48.ck_own.ck, ...), custom_call_target="tpu_custom_call" | custom-call | flops 6643777536 | bytes 16777216 | tf_op jit(solution)/shard_map/pallas_call | solution.py:311
  153.6 1.9 collective-permute-start.16
  155.6 2.4 %collective-permute-done.16.tau_other = bf16[4,11,64,128]{3,2,1,0:T(8,128)(2,1)S(1)} collective-permute-done((bf16[4,11,64,128]{3,2,1,0:T(8,128)(2,1)}, bf16[4,11,64,128]{3,2,1,0:T(8,128)(2,1)S(1)}, u32[]{:S(2)}, u32[]{:S(2)}) %collective-permute-start.16) | collective-permute-done | bytes 720928 | tf_op jit(solution)/shard_map/ppermute | solution.py:576
  157.9 0.9 copy-done.2
  158.8 0.9 shard_map.34
  162.5 0.9 shard_map.35
  166.1 1.0 shard_map.36
  167.8 1.3 collective-permute-start.24
  169.1 1.3 collective-permute-start.25
  170.4 13.8 %collective-permute-done.24.same = bf16[6,64,128]{2,1,0:T(8,128)(2,1)S(1)} collective-permute-done((bf16[6,64,128]{2,1,0:T(8,128)(2,1)}, bf16[6,64,128]{2,1,0:T(8,128)(2,1)S(1)}, u32[]{:S(2)}, u32[]{:S(2)}) %collective-permute-start.24) | collective-permute-done | bytes 98336 | tf_op jit(solution)/shard_map/ppermute | solution.py:592
  184.2 3.8 %collective-permute-done.25.above = bf16[6,64,128]{2,1,0:T(8,128)(2,1)S(1)} collective-permute-done((bf16[6,64,128]{2,1,0:T(8,128)(2,1)}, bf16[6,64,128]{2,1,0:T(8,128)(2,1)S(1)}, u32[]{:S(2)}, u32[]{:S(2)}) %collective-permute-start.25) | collective-permute-done | bytes 98336 | tf_op jit(solution)/shard_map/ppermute | solution.py:592
  188.0 1.9 collective-permute-start.26
  189.9 1.9 collective-permute-done.26.edge_swapped
  191.8 1.0 slice_select_fusion
  192.8 1.3 collective-permute-start.27
  194.2 7.1 %shard_map.37 = (f32[8,2,64,128]{3,2,1,0:T(8,128)}, bf16[6,64,128]{2,1,0:T(8,128)(2,1)}) custom-call(s32[4]{0:T(128)} %pad_add_fusion.sc, bf16[6,64,128]{2,1,0:T(8,128)(2,1)} %copy-done.6, bf16[6,64,128]{2,1,0:T(8,128)(2,1)} %copy-done.7, bf16[6,64,128]{2,1,0:T(8,128)(2,1)} %copy-done.8, ...), custom_call_target="tpu_custom_call", output_to_operand_aliasing={{0}: (9, {})} | custom-call | flops 830472192 | bytes 6291456 | tf_op jit(solution)/shard_map/pallas_call | solution.py:480
  201.9 4.0 %shard_map.38 = bf16[8,64,128]{2,1,0:T(8,128)(2,1)} custom-call(s32[4]{0:T(128)} %pad_add_fusion.sc, bf16[22,64,256]{2,1,0:T(8,128)(2,1)} %get-tuple-element.46.tile, bf16[4,4,64,256]{3,2,1,0:T(8,128)(2,1)} %get-tuple-element.69.edge, bf16[4,4,64,256]{3,2,1,0:T(8,128)(2,1)} %copy-done.4, bf16[1,4,64,256]{3,2,1,0:T(8,128)(2,1)} %copy-done.5, ...), custom_call_target="tpu_custom_call" | custom-call | tf_op jit(solution)/shard_map/pallas_call | solution.py:543
  205.9 17.8 %all_to_all.5 = bf16[8,64,128]{2,1,0:T(8,128)(2,1)S(1)} all-to-all(bf16[8,64,128]{2,1,0:T(8,128)(2,1)} %shard_map.38), channel_id=1, replica_groups=mesh['x'=4,'z'=8,'y'=8,'c'=2] {'z'}, dimensions={0} | all-to-all | bytes 262144 | tf_op jit(solution)/shard_map/all_to_all | solution.py:627
  223.9 0.8 copy.15
  (88 shorter events, 10.1 us)
Async XLA Ops:
  0.0 44.1 %collective-permute-start = (bf16[4,64,576]{2,1,0:T(8,128)(2,1)}, bf16[4,64,576]{2,1,0:T(8,128)(2,1)S(1)}, u32[]{:S(2)}, u32[]{:S(2)}) collective-permute-start(bf16[4,64,576]{2,1,0:T(8,128)(2,1)} %param.5), channel_id=1, source_target_pairs={{0,0},{64,1},{16,16},{80,17},{32,32},{96,33},{48,48},{112,49},{1,6... | collective-permute-start | bytes 884744 | tf_op jit(solution)/shard_map/ppermute | solution.py:595
  1.6 42.5 %collective-permute-start.1 = (bf16[4,64,576]{2,1,0:T(8,128)(2,1)}, bf16[4,64,576]{2,1,0:T(8,128)(2,1)S(1)}, u32[]{:S(2)}, u32[]{:S(2)}) collective-permute-start(bf16[4,64,576]{2,1,0:T(8,128)(2,1)} %param.5), channel_id=1, source_target_pairs={{16,0},{80,1},{32,16},{96,17},{48,32},{112,33},{0,48},{64,49},{17,... | collective-permute-start | bytes 884744 | tf_op jit(solution)/shard_map/ppermute | solution.py:595
  9.5 34.6 %collective-permute-start.2 = (bf16[4,64,576]{2,1,0:T(8,128)(2,1)}, bf16[4,64,576]{2,1,0:T(8,128)(2,1)S(1)}, u32[]{:S(2)}, u32[]{:S(2)}) collective-permute-start(bf16[4,64,576]{2,1,0:T(8,128)(2,1)} %param.5), channel_id=1, source_target_pairs={{32,0},{96,1},{48,16},{112,17},{0,32},{64,33},{16,48},{80,49},{33,... | collective-permute-start | bytes 884744 | tf_op jit(solution)/shard_map/ppermute | solution.py:595
  11.4 32.7 %collective-permute-start.3 = (bf16[4,64,576]{2,1,0:T(8,128)(2,1)}, bf16[4,64,576]{2,1,0:T(8,128)(2,1)S(1)}, u32[]{:S(2)}, u32[]{:S(2)}) collective-permute-start(bf16[4,64,576]{2,1,0:T(8,128)(2,1)} %param.5), channel_id=1, source_target_pairs={{48,0},{112,1},{0,16},{64,17},{16,32},{80,33},{32,48},{96,49},{49,... | collective-permute-start | bytes 884744 | tf_op jit(solution)/shard_map/ppermute | solution.py:595
  44.1 0.7 copy-start.25
  44.1 0.9 copy-start.26
  44.1 0.9 copy-start.27
  45.1 0.7 copy-start.28
  68.4 6.6 %collective-permute-start.5 = (bf16[4,11,64,128]{3,2,1,0:T(8,128)(2,1)}, bf16[4,11,64,128]{3,2,1,0:T(8,128)(2,1)S(1)}, u32[]{:S(2)}, u32[]{:S(2)}) collective-permute-start(bf16[4,11,64,128]{3,2,1,0:T(8,128)(2,1)} %get-tuple-element.52.tau_own), channel_id=1, source_target_pairs={{0,1},{1,0},{2,3},{3,2},{4,5},{5,4},{6,7},{7,6},{8,9},{9,8},{10,11... | collective-permute-start | bytes 2162696 | tf_op jit(solution)/shard_map/ppermute | solution.py:576
  70.7 4.3 %collective-permute-start.6 = (bf16[4,192,192]{2,1,0:T(8,128)(2,1)}, bf16[4,192,192]{2,1,0:T(8,128)(2,1)S(1)}, u32[]{:S(2)}, u32[]{:S(2)}) collective-permute-start(bf16[4,192,192]{2,1,0:T(8,128)(2,1)} %get-tuple-element.48.ck_own.ck), channel_id=1, source_target_pairs={{0,1},{1,0},{2,3},{3,2},{4,5},{5,4},{6,7},{7,6},{8,9},{9,8},{10,11... | collective-permute-start | bytes 884744 | tf_op jit(solution)/shard_map/ppermute | solution.py:576
  72.7 14.9 %collective-permute-start.4 = (bf16[1408,256]{1,0:T(8,128)(2,1)}, bf16[1408,256]{1,0:T(8,128)(2,1)S(1)}, u32[]{:S(2)}, u32[]{:S(2)}) collective-permute-start(bf16[1408,256]{1,0:T(8,128)(2,1)} %get-tuple-element.50), channel_id=1, source_target_pairs={{0,1},{1,128},{128,129},{129,256},{256,257},{257,384},{384,385},{2... | collective-permute-start | bytes 2162696 | tf_op jit(solution)/shard_map/ppermute | solution.py:584
  75.0 0.8 copy-start
  75.0 1.0 copy-start.1
  76.9 2.0 collective-permute-start.7
  77.6 1.4 collective-permute-start.8
  78.3 0.7 collective-permute-start.9
  79.0 0.7 copy-start.22
  79.0 0.7 copy-start.23
  80.6 2.0 collective-permute-start.10
  81.2 1.4 collective-permute-start.11
  81.9 0.7 collective-permute-start.12
  82.6 0.7 copy-start.18
  82.6 0.7 copy-start.20
  83.3 4.3 %copy-start.3 = (bf16[22,64,256]{2,1,0:T(8,128)(2,1)S(1)}, bf16[22,64,256]{2,1,0:T(8,128)(2,1)}, u32[]{:S(2)}) copy-start(bf16[22,64,256]{2,1,0:T(8,128)(2,1)} %get-tuple-element.46.tile) | copy-start | bytes 2162692
  84.3 4.5 %collective-permute-start.13 = (bf16[6,64,128]{2,1,0:T(8,128)(2,1)}, bf16[6,64,128]{2,1,0:T(8,128)(2,1)S(1)}, u32[]{:S(2)}, u32[]{:S(2)}) collective-permute-start(bf16[6,64,128]{2,1,0:T(8,128)(2,1)} %get-tuple-element.57), channel_id=1, source_target_pairs={{256,400},{272,416},{288,432},{304,448},{320,464},{336,480},{352,4... | collective-permute-start | bytes 294920 | tf_op jit(solution)/shard_map/ppermute | solution.py:592
  85.0 37.7 %collective-permute-start.14 = (bf16[6,64,128]{2,1,0:T(8,128)(2,1)}, bf16[6,64,128]{2,1,0:T(8,128)(2,1)S(1)}, u32[]{:S(2)}, u32[]{:S(2)}) collective-permute-start(bf16[6,64,128]{2,1,0:T(8,128)(2,1)} %get-tuple-element.57), channel_id=1, source_target_pairs={{256,384},{272,400},{288,416},{304,432},{320,448},{336,464},{352,4... | collective-permute-start | bytes 294920 | tf_op jit(solution)/shard_map/ppermute | solution.py:592
  86.3 38.5 %collective-permute-start.15 = (bf16[6,64,128]{2,1,0:T(8,128)(2,1)}, bf16[6,64,128]{2,1,0:T(8,128)(2,1)S(1)}, u32[]{:S(2)}, u32[]{:S(2)}) collective-permute-start(bf16[6,64,128]{2,1,0:T(8,128)(2,1)} %get-tuple-element.57), channel_id=1, source_target_pairs={{272,384},{288,400},{304,416},{320,432},{336,448},{352,464},{368,4... | collective-permute-start | bytes 294920 | tf_op jit(solution)/shard_map/ppermute | solution.py:592
  88.8 36.1 %copy-start.15 = (bf16[6,64,128]{2,1,0:T(8,128)(2,1)}, bf16[6,64,128]{2,1,0:T(8,128)(2,1)S(1)}, u32[]{:S(2)}) copy-start(bf16[6,64,128]{2,1,0:T(8,128)(2,1)S(1)} %collective-permute-done.13.below) | copy-start | bytes 294916
  122.7 2.1 copy-start.17
  153.6 4.3 %collective-permute-start.16 = (bf16[4,11,64,128]{3,2,1,0:T(8,128)(2,1)}, bf16[4,11,64,128]{3,2,1,0:T(8,128)(2,1)S(1)}, u32[]{:S(2)}, u32[]{:S(2)}) collective-permute-start(bf16[4,11,64,128]{3,2,1,0:T(8,128)(2,1)} %get-tuple-element.62.tau_own), channel_id=1, source_target_pairs={{0,1},{1,0},{2,3},{3,2},{4,5},{5,4},{6,7},{7,6},{8,9},{9,8},{10,11... | collective-permute-start | bytes 2162696 | tf_op jit(solution)/shard_map/ppermute | solution.py:576
  157.9 0.9 copy-start.2
  159.7 2.0 collective-permute-start.17
  160.4 1.4 collective-permute-start.18
  161.1 0.7 collective-permute-start.19
  163.3 2.0 collective-permute-start.20
  164.0 1.4 collective-permute-start.21
  164.7 0.7 collective-permute-start.22
  166.1 21.9 %copy-start.24 = (bf16[4,4,64,256]{3,2,1,0:T(8,128)(2,1)S(1)}, bf16[4,4,64,256]{3,2,1,0:T(8,128)(2,1)}, u32[]{:S(2)}) copy-start(bf16[4,4,64,256]{3,2,1,0:T(8,128)(2,1)} %get-tuple-element.68) | copy-start | bytes 1572868
  167.1 3.3 %collective-permute-start.23 = (bf16[6,64,128]{2,1,0:T(8,128)(2,1)}, bf16[6,64,128]{2,1,0:T(8,128)(2,1)S(1)}, u32[]{:S(2)}, u32[]{:S(2)}) collective-permute-start(bf16[6,64,128]{2,1,0:T(8,128)(2,1)} %get-tuple-element.67), channel_id=1, source_target_pairs={{256,400},{272,416},{288,432},{304,448},{320,464},{336,480},{352,4... | collective-permute-start | bytes 294920 | tf_op jit(solution)/shard_map/ppermute | solution.py:592
  167.8 16.4 %collective-permute-start.24 = (bf16[6,64,128]{2,1,0:T(8,128)(2,1)}, bf16[6,64,128]{2,1,0:T(8,128)(2,1)S(1)}, u32[]{:S(2)}, u32[]{:S(2)}) collective-permute-start(bf16[6,64,128]{2,1,0:T(8,128)(2,1)} %get-tuple-element.67), channel_id=1, source_target_pairs={{256,384},{272,400},{288,416},{304,432},{320,448},{336,464},{352,4... | collective-permute-start | bytes 294920 | tf_op jit(solution)/shard_map/ppermute | solution.py:592
  169.1 18.9 %collective-permute-start.25 = (bf16[6,64,128]{2,1,0:T(8,128)(2,1)}, bf16[6,64,128]{2,1,0:T(8,128)(2,1)S(1)}, u32[]{:S(2)}, u32[]{:S(2)}) collective-permute-start(bf16[6,64,128]{2,1,0:T(8,128)(2,1)} %get-tuple-element.67), channel_id=1, source_target_pairs={{272,384},{288,400},{304,416},{320,432},{336,448},{352,464},{368,4... | collective-permute-start | bytes 294920 | tf_op jit(solution)/shard_map/ppermute | solution.py:592
  170.4 23.7 %copy-start.6 = (bf16[6,64,128]{2,1,0:T(8,128)(2,1)}, bf16[6,64,128]{2,1,0:T(8,128)(2,1)S(1)}, u32[]{:S(2)}) copy-start(bf16[6,64,128]{2,1,0:T(8,128)(2,1)S(1)} %collective-permute-done.23.below) | copy-start | bytes 294916
  184.2 10.0 %copy-start.7 = (bf16[6,64,128]{2,1,0:T(8,128)(2,1)}, bf16[6,64,128]{2,1,0:T(8,128)(2,1)S(1)}, u32[]{:S(2)}) copy-start(bf16[6,64,128]{2,1,0:T(8,128)(2,1)S(1)} %collective-permute-done.24.same) | copy-start | bytes 294916
  188.0 6.2 %copy-start.8 = (bf16[6,64,128]{2,1,0:T(8,128)(2,1)}, bf16[6,64,128]{2,1,0:T(8,128)(2,1)S(1)}, u32[]{:S(2)}) copy-start(bf16[6,64,128]{2,1,0:T(8,128)(2,1)S(1)} %collective-permute-done.25.above) | copy-start | bytes 294916
  188.0 3.8 %collective-permute-start.26 = (bf16[4,4,64,256]{3,2,1,0:T(8,128)(2,1)S(1)}, bf16[4,4,64,256]{3,2,1,0:T(8,128)(2,1)S(1)}, u32[]{:S(2)}, u32[]{:S(2)}) collective-permute-start(bf16[4,4,64,256]{3,2,1,0:T(8,128)(2,1)S(1)} %copy-done.24), channel_id=1, source_target_pairs={{0,1},{1,0},{2,3},{3,2},{4,5},{5,4},{6,7},{7,6},{8,9},{9,8},{10,11... | collective-permute-start | bytes 1572872 | tf_op jit(solution)/shard_map/ppermute | solution.py:576
  191.8 9.4 %copy-start.4 = (bf16[4,4,64,256]{3,2,1,0:T(8,128)(2,1)}, bf16[4,4,64,256]{3,2,1,0:T(8,128)(2,1)S(1)}, u32[]{:S(2)}) copy-start(bf16[4,4,64,256]{3,2,1,0:T(8,128)(2,1)S(1)} %collective-permute-done.26.edge_swapped) | copy-start | bytes 1572868
  192.8 8.4 %collective-permute-start.27 = (bf16[1,4,64,256]{3,2,1,0:T(8,128)(2,1)S(1)}, bf16[1,4,64,256]{3,2,1,0:T(8,128)(2,1)S(1)}, u32[]{:S(2)}, u32[]{:S(2)}) collective-permute-start(bf16[1,4,64,256]{3,2,1,0:T(8,128)(2,1)S(1)} %slice_select_fusion), channel_id=1, source_target_pairs={{0,128},{128,256},{256,384},{1,129},{129,257},{257,385},{2,130},{1... | collective-permute-start | bytes 393224 | tf_op jit(solution)/shard_map/ppermute | solution.py:610
  201.2 0.7 copy-start.5
  (9 other events, 5.8 us)

commit v3 on v2

--- a/solution.py
+++ b/solution.py
@@ -603,16 +603,18 @@
         received = hand_over(last) if edges is None else None
         packs = [jnp.zeros(PACK, BF16)] * 3
         for p in range(PLANES):
-            if p == PLANES - 1 and edges is not None:
-                mine, others, *packs = lax.optimization_barrier((*edges, *packs))
+            levels, pack = chain(
+                p, edges is not None, place, packs, start, tau, other, kernels, kernels_other, levels
+            )
+            late = p == PLANES - 2 and edges is not None
+            if late:
+                mine, others, pack = lax.optimization_barrier((*edges, pack))
+            if p + 1 < PLANES:
+                packs = upward(pack, p)
+            if late:
                 swapped = swap(others)
                 rows = jnp.where(c == 1, mine[BLOCKS - 1 :], swapped[BLOCKS - 1 :])
                 received = lax.ppermute(rows, "x", [(q, q + 1) for q in range(PLANES - 1)])
-            levels, pack = chain(
-                p, edges is not None, place, packs, start, tau, other, kernels, kernels_other, levels
-            )
-            if p + 1 < PLANES:
-                packs = upward(pack, p)
         return levels, swapped, received
 
     tau, ends, wk, ck, last, tile, start = first_sweeps(place, fetched, rows)

time: 226 us -> 223 us (0.987)
  waiting for transfers between devices: 57.9 us -> 54.5 us
  transfers between devices with their start and end apart: 28 -> 28, of which waited for: 6 -> 5; matrix products, arithmetic and copies ran while one was open for 2% -> 2% of each run, Pallas kernels for 4% -> 4%
where the time goes in v3:
time: 223 us; the launch traced here: 222 us
  Pallas kernels  67.3 us (30%)
  waiting for transfers between devices  54.5 us (24%)
  blocking collectives  46.2 us (21%)
  starting transfers between devices  40.2 us (18%)
  local copies, waits for them, and re-layouts  10.3 us (5%)
  other arithmetic  2.84 us (1%)
    ppermute x18, waiting for transfers between devices, upward(): got.append(lax.ppermute(pack, ('x', 'z'), pairs))  52.1 us
    all_gather x1, blocking collectives, per_device(): rows = lax.all_gather(piece, ('y', 'c'))  28.4 us
    pallas_call x1, Pallas kernels, first_sweeps(): pl.pallas_call(first_kernel, out_shape=[jax.ShapeDtypeStruct(TAU, BF16),...  22.6 us
    pallas_call x1, Pallas kernels, later_sweeps(): pl.pallas_call(later_kernel, out_shape=[jax.ShapeDtypeStruct(TAU, BF16),...  21.2 us
    pallas_call x8, Pallas kernels, chain(): pl.pallas_call(functools.partial(chain_kernel, plane, ending), out_shape=...  19.5 us
    all_to_all x1, blocking collectives, per_device(): got = lax.all_to_all(parts, 'z', 0, 0, tiled=True)  17.8 us
    ppermute x18, starting transfers between devices, upward(): got.append(lax.ppermute(pack, ('x', 'z'), pairs))  14.5 us
    ppermute x4, starting transfers between devices, per_device(): lax.ppermute(weights, ('z', 'c'), kernel_sources(i))  13.9 us
  transfers between devices with their start and end apart: 28, of which 5 were waited for; matrix products, arithmetic and copies ran while one was open for 2% of the time, Pallas kernels for 4%

profile of v3, /device:TPU:6, one launch (start us, length us, event | category | flops | bytes accessed | tf_op | source)
XLA Modules:
  0.0 222.1 jit_solution(4545038632882707268)
XLA Ops:
  0.0 1.6 collective-permute-start
  1.6 7.9 %collective-permute-start.1 = (bf16[4,64,576]{2,1,0:T(8,128)(2,1)}, bf16[4,64,576]{2,1,0:T(8,128)(2,1)S(1)}, u32[]{:S(2)}, u32[]{:S(2)}) collective-permute-start(bf16[4,64,576]{2,1,0:T(8,128)(2,1)} %param.5), channel_id=1, source_target_pairs={{16,0},{80,1},{32,16},{96,17},{48,32},{112,33},{0,48},{64,49},{17,... | collective-permute-start | bytes 884744 | tf_op jit(solution)/shard_map/ppermute | solution.py:595
  9.5 1.9 collective-permute-start.2
  11.4 2.5 %collective-permute-start.3 = (bf16[4,64,576]{2,1,0:T(8,128)(2,1)}, bf16[4,64,576]{2,1,0:T(8,128)(2,1)S(1)}, u32[]{:S(2)}, u32[]{:S(2)}) collective-permute-start(bf16[4,64,576]{2,1,0:T(8,128)(2,1)} %param.5), channel_id=1, source_target_pairs={{48,0},{112,1},{0,16},{64,17},{16,32},{80,33},{32,48},{96,49},{49,... | collective-permute-start | bytes 884744 | tf_op jit(solution)/shard_map/ppermute | solution.py:595
  13.9 1.1 pad_dynamic-slice_fusion
  15.7 28.4 %all_gather.3.source = bf16[16,64,320]{2,1,0:T(8,128)(2,1)} all-gather(bf16[1,64,320]{2,1,0:T(8,128)(2,1)S(1)} %all_gather_reshape.3), channel_id=1, replica_groups=mesh['x'=4,'z'=8,'y'=8,'c'=2] {'y','c'}, dimensions={0}, use_global_device_ids=true | all-gather | bytes 696320 | tf_op jit(solution)/shard_map/all_gather | solution.py:598
  44.2 0.7 copy-done.25
  45.1 0.7 copy-done.28
  45.8 22.6 %shard_map.28 = (bf16[4,11,64,128]{3,2,1,0:T(8,128)(2,1)}, bf16[5,22,64,256]{3,2,1,0:T(8,128)(2,1)}, bf16[4,4,192,192]{3,2,1,0:T(8,128)(2,1)}, bf16[4,192,192]{2...) custom-call(s32[4]{0:T(128)} %pad_add_fusion.sc, ...), custom_call_target="tpu_custom_call" | custom-call | flops 6643777536 | bytes 16777216 | tf_op jit(solution)/shard_map/pallas_call | solution.py:279
  68.4 2.3 %collective-permute-start.5 = (bf16[4,11,64,128]{3,2,1,0:T(8,128)(2,1)}, bf16[4,11,64,128]{3,2,1,0:T(8,128)(2,1)S(1)}, u32[]{:S(2)}, u32[]{:S(2)}) collective-permute-start(bf16[4,11,64,128]{3,2,1,0:T(8,128)(2,1)} %get-tuple-element.50.tau_own), channel_id=1, source_target_pairs={{0,1},{1,0},{2,3},{3,2},{4,5},{5,4},{6,7},{7,6},{8,9},{9,8},{10,11... | collective-permute-start | bytes 2162696 | tf_op jit(solution)/shard_map/ppermute | solution.py:576
  70.7 2.1 collective-permute-start.6
  72.7 2.3 %collective-permute-start.4 = (bf16[1408,256]{1,0:T(8,128)(2,1)}, bf16[1408,256]{1,0:T(8,128)(2,1)S(1)}, u32[]{:S(2)}, u32[]{:S(2)}) collective-permute-start(bf16[1408,256]{1,0:T(8,128)(2,1)} %get-tuple-element.48), channel_id=1, source_target_pairs={{0,1},{1,128},{128,129},{129,256},{256,257},{257,384},{384,385},{2... | collective-permute-start | bytes 2162696 | tf_op jit(solution)/shard_map/ppermute | solution.py:584
  75.0 0.8 broadcast_1_below_same_above.2.below.same.above
  76.0 0.9 shard_map.29
  76.9 0.7 collective-permute-start.7
  77.6 0.7 collective-permute-start.8
  78.3 0.7 collective-permute-start.9
  79.7 0.9 shard_map.30
  80.6 0.7 collective-permute-start.10
  81.2 0.7 collective-permute-start.11
  81.9 0.7 collective-permute-start.12
  83.3 1.0 shard_map.31
  84.3 0.7 collective-permute-start.13
  85.0 1.3 collective-permute-start.14
  86.3 1.3 collective-permute-start.15
  87.6 1.2 bitcast_dynamic-update-slice_fusion.before
  88.8 33.9 %collective-permute-done.14.same = bf16[6,64,128]{2,1,0:T(8,128)(2,1)S(1)} collective-permute-done((bf16[6,64,128]{2,1,0:T(8,128)(2,1)}, bf16[6,64,128]{2,1,0:T(8,128)(2,1)S(1)}, u32[]{:S(2)}, u32[]{:S(2)}) %collective-permute-start.14) | collective-permute-done | bytes 98336 | tf_op jit(solution)/shard_map/ppermute | solution.py:592
  122.7 2.1 collective-permute-done.15.above
  125.5 6.9 %shard_map.32 = (f32[4,11,64,128]{3,2,1,0:T(8,128)}, bf16[6,64,128]{2,1,0:T(8,128)(2,1)}) custom-call(s32[4]{0:T(128)} %pad_add_fusion.sc, bf16[6,64,128]{2,1,0:T(8,128)(2,1)} %copy-done.15, bf16[6,64,128]{2,1,0:T(8,128)(2,1)} %copy-done.17, bf16[6,64,128]{2,1,0:T(8,128)(2,1)} %copy-done.19, ...), custom_call_target="tpu_custom_call", output_to_operand_aliasing={{0}: (9, {})} | custom-call | flops 830472192 | bytes 6291456 | tf_op jit(solution)/shard_map/pallas_call | solution.py:480
  132.4 21.2 %shard_map.33 = (bf16[4,11,64,128]{3,2,1,0:T(8,128)(2,1)}, bf16[4,4,64,256]{3,2,1,0:T(8,128)(2,1)}, bf16[4,4,64,256]{3,2,1,0:T(8,128)(2,1)}) custom-call(s32[4]{0:T(128)} %pad_add_fusion.sc, bf16[4,4,192,192]{3,2,1,0:T(8,128)(2,1)} %get-tuple-element.45.wk, bf16[4,192,192]{2,1,0:T(8,128)(2,1)} %get-tuple-element.46.ck_own.ck, ...), custom_call_target="tpu_custom_call" | custom-call | flops 6643777536 | bytes 16777216 | tf_op jit(solution)/shard_map/pallas_call | solution.py:311
  153.6 1.9 collective-permute-start.16
  155.6 2.4 %collective-permute-done.16.tau_other = bf16[4,11,64,128]{3,2,1,0:T(8,128)(2,1)S(1)} collective-permute-done((bf16[4,11,64,128]{3,2,1,0:T(8,128)(2,1)}, bf16[4,11,64,128]{3,2,1,0:T(8,128)(2,1)S(1)}, u32[]{:S(2)}, u32[]{:S(2)}) %collective-permute-start.16) | collective-permute-done | bytes 720928 | tf_op jit(solution)/shard_map/ppermute | solution.py:576
  157.9 0.9 copy-done.2
  158.8 0.9 shard_map.34
  159.7 0.7 collective-permute-start.17
  162.5 0.9 shard_map.35
  166.1 1.0 shard_map.36
  167.1 2.0 collective-permute-start.23
  169.8 1.3 collective-permute-start.26
  171.1 1.3 collective-permute-start.27
  172.5 1.1 slice_select_fusion
  173.5 1.3 collective-permute-start.24
  174.8 12.1 %collective-permute-done.26.same = bf16[6,64,128]{2,1,0:T(8,128)(2,1)S(1)} collective-permute-done((bf16[6,64,128]{2,1,0:T(8,128)(2,1)}, bf16[6,64,128]{2,1,0:T(8,128)(2,1)S(1)}, u32[]{:S(2)}, u32[]{:S(2)}) %collective-permute-start.26) | collective-permute-done | bytes 98336 | tf_op jit(solution)/shard_map/ppermute | solution.py:592
  187.0 3.9 %collective-permute-done.27.above = bf16[6,64,128]{2,1,0:T(8,128)(2,1)S(1)} collective-permute-done((bf16[6,64,128]{2,1,0:T(8,128)(2,1)}, bf16[6,64,128]{2,1,0:T(8,128)(2,1)S(1)}, u32[]{:S(2)}, u32[]{:S(2)}) %collective-permute-start.27) | collective-permute-done | bytes 98336 | tf_op jit(solution)/shard_map/ppermute | solution.py:592
  191.5 7.1 %shard_map.37 = (f32[8,2,64,128]{3,2,1,0:T(8,128)}, bf16[6,64,128]{2,1,0:T(8,128)(2,1)}) custom-call(s32[4]{0:T(128)} %pad_add_fusion.sc, bf16[6,64,128]{2,1,0:T(8,128)(2,1)} %copy-done.6, bf16[6,64,128]{2,1,0:T(8,128)(2,1)} %copy-done.7, bf16[6,64,128]{2,1,0:T(8,128)(2,1)} %copy-done.8, ...), custom_call_target="tpu_custom_call", output_to_operand_aliasing={{0}: (9, {})} | custom-call | flops 830472192 | bytes 6291456 | tf_op jit(solution)/shard_map/pallas_call | solution.py:480
  199.3 4.0 %shard_map.38 = bf16[8,64,128]{2,1,0:T(8,128)(2,1)} custom-call(s32[4]{0:T(128)} %pad_add_fusion.sc, bf16[22,64,256]{2,1,0:T(8,128)(2,1)} %get-tuple-element.44.tile, bf16[4,4,64,256]{3,2,1,0:T(8,128)(2,1)} %get-tuple-element.67.edge, bf16[4,4,64,256]{3,2,1,0:T(8,128)(2,1)} %copy-done.4, bf16[1,4,64,256]{3,2,1,0:T(8,128)(2,1)} %copy-done.5, ...), custom_call_target="tpu_custom_call" | custom-call | tf_op jit(solution)/shard_map/pallas_call | solution.py:543
  203.3 17.8 %all_to_all.5 = bf16[8,64,128]{2,1,0:T(8,128)(2,1)S(1)} all-to-all(bf16[8,64,128]{2,1,0:T(8,128)(2,1)} %shard_map.38), channel_id=1, replica_groups=mesh['x'=4,'z'=8,'y'=8,'c'=2] {'z'}, dimensions={0} | all-to-all | bytes 262144 | tf_op jit(solution)/shard_map/all_to_all | solution.py:629
  221.3 0.8 copy.15
  (88 shorter events, 10.1 us)
Async XLA Ops:
  0.0 44.1 %collective-permute-start = (bf16[4,64,576]{2,1,0:T(8,128)(2,1)}, bf16[4,64,576]{2,1,0:T(8,128)(2,1)S(1)}, u32[]{:S(2)}, u32[]{:S(2)}) collective-permute-start(bf16[4,64,576]{2,1,0:T(8,128)(2,1)} %param.5), channel_id=1, source_target_pairs={{0,0},{64,1},{16,16},{80,17},{32,32},{96,33},{48,48},{112,49},{1,6... | collective-permute-start | bytes 884744 | tf_op jit(solution)/shard_map/ppermute | solution.py:595
  1.6 42.5 %collective-permute-start.1 = (bf16[4,64,576]{2,1,0:T(8,128)(2,1)}, bf16[4,64,576]{2,1,0:T(8,128)(2,1)S(1)}, u32[]{:S(2)}, u32[]{:S(2)}) collective-permute-start(bf16[4,64,576]{2,1,0:T(8,128)(2,1)} %param.5), channel_id=1, source_target_pairs={{16,0},{80,1},{32,16},{96,17},{48,32},{112,33},{0,48},{64,49},{17,... | collective-permute-start | bytes 884744 | tf_op jit(solution)/shard_map/ppermute | solution.py:595
  9.5 34.6 %collective-permute-start.2 = (bf16[4,64,576]{2,1,0:T(8,128)(2,1)}, bf16[4,64,576]{2,1,0:T(8,128)(2,1)S(1)}, u32[]{:S(2)}, u32[]{:S(2)}) collective-permute-start(bf16[4,64,576]{2,1,0:T(8,128)(2,1)} %param.5), channel_id=1, source_target_pairs={{32,0},{96,1},{48,16},{112,17},{0,32},{64,33},{16,48},{80,49},{33,... | collective-permute-start | bytes 884744 | tf_op jit(solution)/shard_map/ppermute | solution.py:595
  11.4 32.7 %collective-permute-start.3 = (bf16[4,64,576]{2,1,0:T(8,128)(2,1)}, bf16[4,64,576]{2,1,0:T(8,128)(2,1)S(1)}, u32[]{:S(2)}, u32[]{:S(2)}) collective-permute-start(bf16[4,64,576]{2,1,0:T(8,128)(2,1)} %param.5), channel_id=1, source_target_pairs={{48,0},{112,1},{0,16},{64,17},{16,32},{80,33},{32,48},{96,49},{49,... | collective-permute-start | bytes 884744 | tf_op jit(solution)/shard_map/ppermute | solution.py:595
  44.1 0.7 copy-start.25
  44.1 0.9 copy-start.26
  44.1 0.9 copy-start.27
  45.1 0.7 copy-start.28
  68.4 6.6 %collective-permute-start.5 = (bf16[4,11,64,128]{3,2,1,0:T(8,128)(2,1)}, bf16[4,11,64,128]{3,2,1,0:T(8,128)(2,1)S(1)}, u32[]{:S(2)}, u32[]{:S(2)}) collective-permute-start(bf16[4,11,64,128]{3,2,1,0:T(8,128)(2,1)} %get-tuple-element.50.tau_own), channel_id=1, source_target_pairs={{0,1},{1,0},{2,3},{3,2},{4,5},{5,4},{6,7},{7,6},{8,9},{9,8},{10,11... | collective-permute-start | bytes 2162696 | tf_op jit(solution)/shard_map/ppermute | solution.py:576
  70.7 4.3 %collective-permute-start.6 = (bf16[4,192,192]{2,1,0:T(8,128)(2,1)}, bf16[4,192,192]{2,1,0:T(8,128)(2,1)S(1)}, u32[]{:S(2)}, u32[]{:S(2)}) collective-permute-start(bf16[4,192,192]{2,1,0:T(8,128)(2,1)} %get-tuple-element.46.ck_own.ck), channel_id=1, source_target_pairs={{0,1},{1,0},{2,3},{3,2},{4,5},{5,4},{6,7},{7,6},{8,9},{9,8},{10,11... | collective-permute-start | bytes 884744 | tf_op jit(solution)/shard_map/ppermute | solution.py:576
  72.7 14.9 %collective-permute-start.4 = (bf16[1408,256]{1,0:T(8,128)(2,1)}, bf16[1408,256]{1,0:T(8,128)(2,1)S(1)}, u32[]{:S(2)}, u32[]{:S(2)}) collective-permute-start(bf16[1408,256]{1,0:T(8,128)(2,1)} %get-tuple-element.48), channel_id=1, source_target_pairs={{0,1},{1,128},{128,129},{129,256},{256,257},{257,384},{384,385},{2... | collective-permute-start | bytes 2162696 | tf_op jit(solution)/shard_map/ppermute | solution.py:584
  75.0 0.8 copy-start
  75.0 1.0 copy-start.1
  76.9 2.0 collective-permute-start.7
  77.6 1.4 collective-permute-start.8
  78.3 0.7 collective-permute-start.9
  79.0 0.7 copy-start.22
  79.0 0.7 copy-start.23
  80.6 2.0 collective-permute-start.10
  81.2 1.4 collective-permute-start.11
  81.9 0.7 collective-permute-start.12
  82.6 0.7 copy-start.18
  82.6 0.7 copy-start.20
  83.3 4.3 %copy-start.3 = (bf16[22,64,256]{2,1,0:T(8,128)(2,1)S(1)}, bf16[22,64,256]{2,1,0:T(8,128)(2,1)}, u32[]{:S(2)}) copy-start(bf16[22,64,256]{2,1,0:T(8,128)(2,1)} %get-tuple-element.44.tile) | copy-start | bytes 2162692
  84.3 4.5 %collective-permute-start.13 = (bf16[6,64,128]{2,1,0:T(8,128)(2,1)}, bf16[6,64,128]{2,1,0:T(8,128)(2,1)S(1)}, u32[]{:S(2)}, u32[]{:S(2)}) collective-permute-start(bf16[6,64,128]{2,1,0:T(8,128)(2,1)} %get-tuple-element.55), channel_id=1, source_target_pairs={{256,400},{272,416},{288,432},{304,448},{320,464},{336,480},{352,4... | collective-permute-start | bytes 294920 | tf_op jit(solution)/shard_map/ppermute | solution.py:592
  85.0 37.7 %collective-permute-start.14 = (bf16[6,64,128]{2,1,0:T(8,128)(2,1)}, bf16[6,64,128]{2,1,0:T(8,128)(2,1)S(1)}, u32[]{:S(2)}, u32[]{:S(2)}) collective-permute-start(bf16[6,64,128]{2,1,0:T(8,128)(2,1)} %get-tuple-element.55), channel_id=1, source_target_pairs={{256,384},{272,400},{288,416},{304,432},{320,448},{336,464},{352,4... | collective-permute-start | bytes 294920 | tf_op jit(solution)/shard_map/ppermute | solution.py:592
  86.3 38.5 %collective-permute-start.15 = (bf16[6,64,128]{2,1,0:T(8,128)(2,1)}, bf16[6,64,128]{2,1,0:T(8,128)(2,1)S(1)}, u32[]{:S(2)}, u32[]{:S(2)}) collective-permute-start(bf16[6,64,128]{2,1,0:T(8,128)(2,1)} %get-tuple-element.55), channel_id=1, source_target_pairs={{272,384},{288,400},{304,416},{320,432},{336,448},{352,464},{368,4... | collective-permute-start | bytes 294920 | tf_op jit(solution)/shard_map/ppermute | solution.py:592
  88.8 36.1 %copy-start.15 = (bf16[6,64,128]{2,1,0:T(8,128)(2,1)}, bf16[6,64,128]{2,1,0:T(8,128)(2,1)S(1)}, u32[]{:S(2)}) copy-start(bf16[6,64,128]{2,1,0:T(8,128)(2,1)S(1)} %collective-permute-done.13.below) | copy-start | bytes 294916
  122.7 2.1 copy-start.17
  153.6 4.3 %collective-permute-start.16 = (bf16[4,11,64,128]{3,2,1,0:T(8,128)(2,1)}, bf16[4,11,64,128]{3,2,1,0:T(8,128)(2,1)S(1)}, u32[]{:S(2)}, u32[]{:S(2)}) collective-permute-start(bf16[4,11,64,128]{3,2,1,0:T(8,128)(2,1)} %get-tuple-element.60.tau_own), channel_id=1, source_target_pairs={{0,1},{1,0},{2,3},{3,2},{4,5},{5,4},{6,7},{7,6},{8,9},{9,8},{10,11... | collective-permute-start | bytes 2162696 | tf_op jit(solution)/shard_map/ppermute | solution.py:576
  157.9 0.9 copy-start.2
  159.7 2.0 collective-permute-start.17
  160.4 1.4 collective-permute-start.18
  161.1 0.7 collective-permute-start.19
  163.3 2.0 collective-permute-start.20
  164.0 1.4 collective-permute-start.21
  164.7 0.7 collective-permute-start.22
  165.4 0.7 copy-start.14
  166.1 1.0 copy-start.24
  167.1 5.3 %collective-permute-start.23 = (bf16[4,4,64,256]{3,2,1,0:T(8,128)(2,1)S(1)}, bf16[4,4,64,256]{3,2,1,0:T(8,128)(2,1)S(1)}, u32[]{:S(2)}, u32[]{:S(2)}) collective-permute-start(bf16[4,4,64,256]{3,2,1,0:T(8,128)(2,1)S(1)} %copy-done.24), channel_id=1, source_target_pairs={{0,1},{1,0},{2,3},{3,2},{4,5},{5,4},{6,7},{7,6},{8,9},{9,8},{10,11... | collective-permute-start | bytes 1572872 | tf_op jit(solution)/shard_map/ppermute | solution.py:576
  169.2 5.7 %collective-permute-start.25 = (bf16[6,64,128]{2,1,0:T(8,128)(2,1)}, bf16[6,64,128]{2,1,0:T(8,128)(2,1)S(1)}, u32[]{:S(2)}, u32[]{:S(2)}) collective-permute-start(bf16[6,64,128]{2,1,0:T(8,128)(2,1)} %get-tuple-element.68), channel_id=1, source_target_pairs={{256,400},{272,416},{288,432},{304,448},{320,464},{336,480},{352,4... | collective-permute-start | bytes 294920 | tf_op jit(solution)/shard_map/ppermute | solution.py:592
  169.8 17.1 %collective-permute-start.26 = (bf16[6,64,128]{2,1,0:T(8,128)(2,1)}, bf16[6,64,128]{2,1,0:T(8,128)(2,1)S(1)}, u32[]{:S(2)}, u32[]{:S(2)}) collective-permute-start(bf16[6,64,128]{2,1,0:T(8,128)(2,1)} %get-tuple-element.68), channel_id=1, source_target_pairs={{256,384},{272,400},{288,416},{304,432},{320,448},{336,464},{352,4... | collective-permute-start | bytes 294920 | tf_op jit(solution)/shard_map/ppermute | solution.py:592
  171.1 19.7 %collective-permute-start.27 = (bf16[6,64,128]{2,1,0:T(8,128)(2,1)}, bf16[6,64,128]{2,1,0:T(8,128)(2,1)S(1)}, u32[]{:S(2)}, u32[]{:S(2)}) collective-permute-start(bf16[6,64,128]{2,1,0:T(8,128)(2,1)} %get-tuple-element.68), channel_id=1, source_target_pairs={{272,384},{288,400},{304,416},{320,432},{336,448},{352,464},{368,4... | collective-permute-start | bytes 294920 | tf_op jit(solution)/shard_map/ppermute | solution.py:592
  172.4 26.1 %copy-start.4 = (bf16[4,4,64,256]{3,2,1,0:T(8,128)(2,1)}, bf16[4,4,64,256]{3,2,1,0:T(8,128)(2,1)S(1)}, u32[]{:S(2)}) copy-start(bf16[4,4,64,256]{3,2,1,0:T(8,128)(2,1)S(1)} %collective-permute-done.23.edge_swapped) | copy-start | bytes 1572868
  173.5 25.1 %collective-permute-start.24 = (bf16[1,4,64,256]{3,2,1,0:T(8,128)(2,1)S(1)}, bf16[1,4,64,256]{3,2,1,0:T(8,128)(2,1)S(1)}, u32[]{:S(2)}, u32[]{:S(2)}) collective-permute-start(bf16[1,4,64,256]{3,2,1,0:T(8,128)(2,1)S(1)} %slice_select_fusion), channel_id=1, source_target_pairs={{0,128},{128,256},{256,384},{1,129},{129,257},{257,385},{2,130},{1... | collective-permute-start | bytes 393224 | tf_op jit(solution)/shard_map/ppermute | solution.py:617
  174.8 16.1 %copy-start.6 = (bf16[6,64,128]{2,1,0:T(8,128)(2,1)}, bf16[6,64,128]{2,1,0:T(8,128)(2,1)S(1)}, u32[]{:S(2)}) copy-start(bf16[6,64,128]{2,1,0:T(8,128)(2,1)S(1)} %collective-permute-done.25.below) | copy-start | bytes 294916
  187.0 3.9 %copy-start.7 = (bf16[6,64,128]{2,1,0:T(8,128)(2,1)}, bf16[6,64,128]{2,1,0:T(8,128)(2,1)S(1)}, u32[]{:S(2)}) copy-start(bf16[6,64,128]{2,1,0:T(8,128)(2,1)S(1)} %collective-permute-done.26.same) | copy-start | bytes 294916
  198.6 0.7 copy-start.5
  (9 other events, 5.8 us)
